TPU v7x, 512 devices: a whole 4x8x8 slice. The times are simulated.
512 devices in a mesh: lat: 16 (over x, y_lo, core), lon: 32 (over y_hi, z).
Axes of the slice: x: 4, y: 8 (y_hi: 4, y_lo: 2; y = y_hi * 2 + y_lo), z: 8, core: 2. Of those that a mesh axis runs over, the one named last changes fastest.
Arguments:
- fields: bfloat16 [256, 512, 384], P('lat', 'lon'), may hold values from -6 to 6
- spectral_gain: float32 [192, 384], P(None, 'lon'), may hold values from -4 to 4
- stencil_one: bfloat16 [256, 3, 5, 13], P('lat'), may hold values from -1 to 1
- stencil_two: bfloat16 [256, 3, 5, 13], P('lat'), may hold values from -1 to 1
- cycle_reach: int32 [256], P('lat'), may hold values from 1 to 6, as said below
- mix_one: bfloat16 [3, 384, 384], replicated, may hold values from -0.1875 to 0.1875
- mix_two: bfloat16 [3, 384, 384], replicated, may hold values from -0.1875 to 0.1875
- norm_gain: float32 [384], replicated, may hold values from 0.1 to 1.9
- w_in: bfloat16 [384, 768], replicated, may hold values from -0.3125 to 0.3125
- w_out: bfloat16 [768, 384], replicated, may hold values from -0.21875 to 0.21875
Outputs:
- block_out: bfloat16 [256, 512, 384], P('lat', 'lon')
Inputs may be any that keep to these rules, and one draw needn't show every extreme that they name: `cycle_reach`: the cycles nearest the two poles reach 6 cells.
All inputs are finite; a program needn't handle non-finite values.
Results may differ from a plain program's by a relative error of at most 0.013.
Values may be sent and summed in bfloat16 or wider, within the bound.
No kernel may reach another device: no remote copies, remote signals or barrier semaphores. Data moves between devices by JAX's collectives and lax.ppermute only.
A program may use at most 64 MiB of HBM per device.

v0:
```python
import math

import jax
import jax.numpy as jnp
from jax import lax
from jax.sharding import PartitionSpec as P

LM_DEV = 12
LB = 16
RLAT = 2
RLON = 6


def extended_2(cells, sides, width, closed):
    for axis, dim in sides:
        count = lax.axis_size(axis)
        ends = count if closed else count - 1
        head = lax.slice_in_dim(cells, 0, width, axis=dim)
        tail = lax.slice_in_dim(cells, cells.shape[dim] - width, cells.shape[dim], axis=dim)
        cells = jnp.concatenate(
            [
                lax.ppermute(tail, axis, [(i, (i + 1) % count) for i in range(ends)]),
                cells,
                lax.ppermute(head, axis, [((i + 1) % count, i) for i in range(ends)]),
            ],
            axis=dim,
        )
    return cells


def legendre_table(colatitude, orders, degrees):
    order_vals = orders.astype(jnp.float32)
    counter = jnp.arange(1, degrees + 1, dtype=jnp.int32).astype(jnp.float32)
    factors = jnp.log((2.0 * counter - 1.0) / (2.0 * counter))
    partial_sum = jnp.sum(
        jnp.where(counter[None, :] <= order_vals[:, None], factors[None, :], 0.0), axis=1
    )
    log_sine = jnp.log(jnp.sin(colatitude))
    start_log = 0.5 * jnp.log((2.0 * order_vals + 1.0) / (4.0 * math.pi)) + 0.5 * partial_sum
    diagonal = jnp.exp(start_log[None, :] + order_vals[None, :] * log_sine[:, None])
    cosine = jnp.cos(colatitude)[:, None]
    squared_m = order_vals * order_vals

    def advance(state_pair, degree):
        previous, earlier = state_pair
        degree_f = degree.astype(jnp.float32)
        coef_up = jnp.sqrt(
            jnp.maximum(4.0 * degree_f * degree_f - 1.0, 0.0)
            / jnp.maximum(degree_f * degree_f - squared_m, 1.0)
        )
        degree_b = degree_f - 1.0
        coef_down = jnp.sqrt(
            jnp.maximum(degree_b * degree_b - squared_m, 0.0)
            / jnp.maximum(4.0 * degree_b * degree_b - 1.0, 1.0)
        )
        entry = coef_up[None, :] * (cosine * previous - coef_down[None, :] * earlier)
        entry = jnp.where(degree == orders[None, :], diagonal, entry)
        entry = jnp.where(degree < orders[None, :], jnp.zeros_like(entry), entry)
        return ((entry, previous), entry)

    zero_field = jnp.zeros((colatitude.shape[0], orders.shape[0]), jnp.float32)
    _, stacked = lax.scan(
        advance, (zero_field, zero_field), jnp.arange(degrees, dtype=jnp.int32), unroll=8
    )
    return stacked


def fourier_angles(orders, lon_count):
    cells = jnp.arange(lon_count, dtype=jnp.int32)
    product = orders[:, None] * cells[None, :] % lon_count
    return 2.0 * math.pi / lon_count * product.astype(jnp.float32)


def forward_orders(spectra_in, plm_group, lowest):
    degree_count = plm_group.shape[0]
    full_shape = spectra_in.shape[:3] + (degree_count,)
    zeros_block = jnp.zeros(spectra_in.shape[:3] + (LB,), jnp.float32)

    def forward_advance_block(number, running):
        degree_start = number * LB

        def forward_compute(unused):
            plm_block = lax.dynamic_slice_in_dim(plm_group, degree_start, LB, 0)
            return jnp.einsum(
                "cqgi,lig->cqgl", spectra_in, plm_block, precision=lax.Precision.HIGHEST
            )

        def forward_skipped(unused):
            return zeros_block

        portion = lax.cond(degree_start + LB <= lowest, forward_skipped, forward_compute, 0)
        return lax.dynamic_update_slice_in_dim(running, portion, degree_start, 3)

    return lax.fori_loop(
        0, degree_count // LB, forward_advance_block, jnp.zeros(full_shape, jnp.float32)
    )


def inverse_orders(harmonics, plm_group, lowest):
    degree_count = plm_group.shape[0]
    full_shape = harmonics.shape[:3] + (plm_group.shape[1],)

    def inverse_advance_block(number, running):
        degree_start = number * LB

        def inverse_compute(sofar):
            plm_block = lax.dynamic_slice_in_dim(plm_group, degree_start, LB, 0)
            portion = lax.dynamic_slice_in_dim(harmonics, degree_start, LB, 3)
            return sofar + jnp.einsum(
                "cqgl,lig->cqgi", portion, plm_block, precision=lax.Precision.HIGHEST
            )

        def inverse_skipped(sofar):
            return sofar

        return lax.cond(degree_start + LB <= lowest, inverse_skipped, inverse_compute, running)

    return lax.fori_loop(
        0, degree_count // LB, inverse_advance_block, jnp.zeros(full_shape, jnp.float32)
    )


def disco_layer(field, stencil, mixing, cycle_reach):
    lat_rows, lon_cols, channels = field.shape
    rimmed = extended_2(field, (("lat", 0),), RLAT, False)
    extended = extended_2(rimmed, (("lon", 1),), RLON, True)
    tap_count = 2 * RLON + 1
    width_ext = lon_cols + 2 * RLON
    offsets = jnp.arange(tap_count, dtype=jnp.int32) - RLON
    inside = (jnp.abs(offsets)[None, :] <= cycle_reach[:, None]).astype(jnp.bfloat16)
    masked = stencil * inside[:, None, None, :]
    tap_ids = jnp.arange(tap_count, dtype=jnp.int32)
    out_ids = jnp.arange(lon_cols, dtype=jnp.int32)
    in_ids = jnp.arange(width_ext, dtype=jnp.int32)
    one_hot = (in_ids[None, None, :] - out_ids[None, :, None] == tap_ids[:, None, None]).astype(
        jnp.bfloat16
    )
    banded = jnp.einsum(
        "akdt,tjn->akdjn", masked, one_hot, preferred_element_type=jnp.float32
    ).astype(jnp.bfloat16)
    stacked = jnp.stack(
        [extended[row_shift : row_shift + lat_rows] for row_shift in range(2 * RLAT + 1)], axis=1
    )
    gathered = jnp.einsum(
        "akdjn,adnc->akjc", banded, stacked, preferred_element_type=jnp.float32
    ).astype(jnp.bfloat16)
    return jnp.einsum("akjc,kce->aje", gathered, mixing, preferred_element_type=jnp.float32)


def finish(stream, second, norm_gain, w_in, w_out):
    summed = stream.astype(jnp.float32) + second
    center = summed - jnp.mean(summed, axis=-1, keepdims=True)
    spread = jnp.mean(center * center, axis=-1, keepdims=True)
    normed = (center * lax.rsqrt(spread + 1e-05) * norm_gain).astype(jnp.bfloat16)
    shape_out = normed.shape
    flat = normed.reshape(-1, shape_out[-1])
    hidden = jax.nn.gelu(jnp.dot(flat, w_in, preferred_element_type=jnp.float32)).astype(
        jnp.bfloat16
    )
    update = jnp.dot(hidden, w_out, preferred_element_type=jnp.float32).reshape(shape_out)
    return (stream.astype(jnp.float32) + update).astype(jnp.bfloat16)


def local(
    fields,
    spectral_gain,
    stencil_one,
    stencil_two,
    cycle_reach,
    mix_one,
    mix_two,
    norm_gain,
    w_in,
    w_out,
):
    lat_rows, lon_cols, channels = fields.shape
    lat_parts = lax.axis_size("lat")
    lon_parts = lax.axis_size("lon")
    total_rows = lat_rows * lat_parts
    total_cols = lon_cols * lon_parts
    order_share = LM_DEV
    degree_total = LM_DEV * lat_parts
    orders = jnp.arange(degree_total, dtype=jnp.int32)
    lat_place = lax.axis_index("lat")
    own_orders = lax.dynamic_slice_in_dim(orders, lat_place * order_share, order_share, 0)
    colatitude = (
        math.pi * (jnp.arange(total_rows, dtype=jnp.int32).astype(jnp.float32) + 0.5) / total_rows
    )
    quad_weight = math.pi / total_rows * (2.0 * math.pi / total_cols) * jnp.sin(colatitude)
    whole_table = legendre_table(colatitude, own_orders, degree_total)
    angles = fourier_angles(orders, total_cols)
    forward_table = jnp.stack([jnp.cos(angles).T, -jnp.sin(angles).T], axis=1).astype(jnp.bfloat16)
    doubling = jnp.where(orders == 0, 1.0, 2.0).astype(jnp.float32)[:, None]
    inverse_table = jnp.stack([doubling * jnp.cos(angles), -doubling * jnp.sin(angles)], axis=0)
    gain_cols = spectral_gain.T
    turned = jnp.transpose(fields, (0, 2, 1))
    spectra = jnp.einsum(
        "acn,nrm->crma",
        lax.all_to_all(turned, "lon", split_axis=1, concat_axis=2, tiled=True),
        forward_table,
        preferred_element_type=jnp.float32,
    )
    weighted = (
        lax.all_to_all(
            spectra.astype(jnp.bfloat16), "lat", split_axis=2, concat_axis=3, tiled=True
        ).astype(spectra.dtype)
        * quad_weight[None, None, None, :]
    )
    lowest = jnp.min(own_orders)
    harmonics = forward_orders(weighted, whole_table, lowest) * gain_cols[:, None, None, :]
    results = inverse_orders(harmonics, whole_table, lowest)
    grid_part = jnp.einsum(
        "crma,rmn->acn",
        lax.all_to_all(
            results.astype(jnp.bfloat16), "lat", split_axis=3, concat_axis=2, tiled=True
        ).astype(results.dtype),
        inverse_table,
        precision=lax.Precision.HIGHEST,
    )
    sector_grid = grid_part.astype(jnp.bfloat16)
    spectral = lax.all_to_all(sector_grid, "lon", split_axis=2, concat_axis=1, tiled=True)
    spectral = jnp.transpose(spectral, (0, 2, 1))
    first = disco_layer(fields, stencil_one, mix_one, cycle_reach)
    stream = (fields.astype(jnp.float32) + spectral.astype(jnp.float32) + first).astype(
        jnp.bfloat16
    )
    second = disco_layer(stream, stencil_two, mix_two, cycle_reach)
    return finish(stream, second, norm_gain, w_in, w_out)


def solution(mesh):
    in_specs = (
        P("lat", "lon", None),
        P(None, "lon"),
        P("lat", None, None, None),
        P("lat", None, None, None),
        P("lat"),
        P(),
        P(),
        P(),
        P(),
        P(),
    )
    out_specs = P("lat", "lon", None)
    return jax.shard_map(local, mesh=mesh, in_specs=in_specs, out_specs=out_specs, check_vma=False)
```

profile of v0, /device:TPU:1, one launch (start us, length us, event | category | flops | bytes accessed | tf_op | source)
XLA Modules:
  0.0 601.2 jit_solution(11480769585414520628)
XLA Ops:
  6.9 16.5 %all-to-all-start = ((bf16[32,2,1536]{2,1,0:T(2,128)(2,1)}), bf16[32,2,1536]{2,1,0:T(2,128)(2,1)S(1)}, u32[]{:S(2)}, u32[]{:S(2)}) async-start(bf16[32,2,1536]{2,1,0:T(2,128)(2,1)} %reshape.553), calls=%async_computation | async-start | bytes 393216 | tf_op jit(solution)/shard_map/all_to_all | solution.py:199
  31.4 297.0 %while.50 = (s32[]{:T(128)}, f32[256,12]{0,1:T(8,128)S(1)}, f32[256,12]{0,1:T(8,128)S(1)}, f32[24,8,256,12]{2,3,1,0:T(8,128)}, s32[24,8]{0,1:T(8,128)S(1)}, /*in...) while((s32[]{:T(128)}, f32[256,12]{0,1:T(8,128)S(1)}, ...), condition=%wide.region_3.4_spmd.clone.clone, body=%wide.region_2.3_spmd.clone.clone.sunk | while | flops 431714 | bytes 777551 | solution.py:62
  37.2 5.0 broadcast_compare_fusion.17
  49.6 5.0 broadcast_compare_fusion.17
  62.0 5.0 broadcast_compare_fusion.17
  74.4 5.0 broadcast_compare_fusion.17
  86.7 5.0 broadcast_compare_fusion.17
  99.1 5.0 broadcast_compare_fusion.17
  111.5 5.0 broadcast_compare_fusion.17
  123.9 5.0 broadcast_compare_fusion.17
  136.2 5.0 broadcast_compare_fusion.17
  148.6 5.0 broadcast_compare_fusion.17
  185.7 5.0 broadcast_compare_fusion.17
  210.5 5.0 broadcast_compare_fusion.17
  222.8 5.0 broadcast_compare_fusion.17
  247.6 5.0 broadcast_compare_fusion.17
  260.0 5.0 broadcast_compare_fusion.17
  272.3 5.0 broadcast_compare_fusion.17
  284.7 5.0 broadcast_compare_fusion.17
  297.1 5.0 broadcast_compare_fusion.17
  309.5 5.0 broadcast_compare_fusion.17
  321.8 5.0 broadcast_compare_fusion.17
  341.7 6.8 %collective-permute-start.3 = (bf16[20,6,384]{2,1,0:T(8,128)(2,1)}, bf16[20,6,384]{2,1,0:T(8,128)(2,1)}, u32[]{:S(2)}, u32[]{:S(2)}) collective-permute-start(bf16[20,6,384]{2,1,0:T(8,128)(2,1)} %get-tuple-element.633), channel_id=1, source_target_pairs={{1,0},{2,1},{3,2},{4,3},{5,4},{6,5},{7,6},{8,7},{9,8},{10,9},{11,1... | collective-permute-start | bytes 276488 | tf_op jit(solution)/shard_map/ppermute | solution.py:24
  359.2 7.3 %all-to-all-start.1 = ((bf16[16,2,2304]{2,1,0:T(2,128)(2,1)}), bf16[16,2,2304]{2,1,0:T(2,128)(2,1)S(1)}, u32[]{:S(2)}, u32[]{:S(2)}) async-start(bf16[16,2,2304]{2,1,0:T(2,128)(2,1)} %reshape.555), calls=%async_computation.1 | async-start | bytes 294912 | tf_op jit(solution)/shard_map/all_to_all | solution.py:204
  377.9 5.3 copy.102
  386.3 77.5 %while.48 = (s32[]{:T(128)}, f32[12,2,12,192]{3,0,1,2:T(8,128)S(1)}, s32[]{:T(128)}, f32[192,256,12]{1,0,2:T(8,128)}, f32[12,2,12,256]{3,0,1,2:T(8,128)S(1)}, /*index=5*/s32[]{:T(128)}, s32[]{:T(128)}, s32[]{:T(128)}, s32[]{:T(128)}) while((s32[]{:T(128)}, f32[12,2,12,192]{3,0,1,2:T(8,128)S(1)}, s32[]{:T(128)}, f32[192,256,12]{1,0,2:T(8,128)}, ...), condition=%wide.region_7.8_spmd, body=%wide.region_4.7_spmd.sunk | while | flops 14155788 | bytes 583919 | solution.py:94
  463.9 25.8 %while.49 = (s32[]{:T(128)}, f32[12,2,12,256]{3,0,1,2:T(8,128)S(1)}, s32[]{:T(128)}, f32[192,256,12]{1,0,2:T(8,128)}, f32[12,2,12,192]{3,0,1,2:T(8,128)S(1)}, /*index=5*/s32[]{:T(128)}, s32[]{:T(128)}) while((s32[]{:T(128)}, f32[12,2,12,256]{3,0,1,2:T(8,128)S(1)}, s32[]{:T(128)}, f32[192,256,12]{1,0,2:T(8,128)}, ...), condition=%wide.region_11.12_spmd, body=%wide.region_8.11_spmd.sunk | while | flops 14229513 | bytes 1082557 | solution.py:118
  509.3 5.8 copy.136
  525.4 9.1 %all-to-all-start.3 = ((bf16[32,2,1536]{2,1,0:T(2,128)(2,1)}), bf16[32,2,1536]{2,1,0:T(2,128)(2,1)S(1)}, u32[]{:S(2)}, u32[]{:S(2)}) async-start(bf16[32,2,1536]{2,1,0:T(2,128)(2,1)} %reshape.559), calls=%async_computation.3 | async-start | bytes 393216 | tf_op jit(solution)/shard_map/all_to_all | solution.py:221
  536.3 10.3 %all-to-all-done.3 = bf16[32,2,1536]{2,1,0:T(2,128)(2,1)S(1)} async-done(((bf16[32,2,1536]{2,1,0:T(2,128)(2,1)}), bf16[32,2,1536]{2,1,0:T(2,128)(2,1)S(1)}, u32[]{:S(2)}, u32[]{:S(2)}) %all-to-all-start.3) | async-done | bytes 196640 | tf_op jit(solution)/shard_map/all_to_all | solution.py:221
  552.7 7.1 %copy.112 = f32[16,32,12,16]{2,1,3,0:T(8,128)} copy(f32[16,32,12,16]{3,1,0,2:T(8,128)} %bitcast.287) | data formatting | bytes 786432 | tf_op jit(solution)/shard_map/convert_element_type | solution.py:224
  580.1 6.7 %collective-permute-start.7 = (bf16[20,6,384]{2,1,0:T(8,128)(2,1)S(1)}, bf16[20,6,384]{2,1,0:T(8,128)(2,1)S(1)}, u32[]{:S(2)}, u32[]{:S(2)}) collective-permute-start(bf16[20,6,384]{2,1,0:T(8,128)(2,1)S(1)} %get-tuple-element.631), channel_id=1, source_target_pairs={{1,0},{2,1},{3,2},{4,3},{5,4},{6,5},{7,6},{8,7},{9,8},{10,9},{11,1... | collective-permute-start | bytes 276488 | tf_op jit(solution)/shard_map/ppermute | solution.py:24
  (533 shorter events, 334.9 us)
Async XLA Ops:
  0.0 595.3 %copy-start = (bf16[3,384,384]{2,1,0:T(8,128)(2,1)S(1)}, bf16[3,384,384]{2,1,0:T(8,128)(2,1)}, u32[]{:S(2)}) copy-start(bf16[3,384,384]{2,1,0:T(8,128)(2,1)} %param.26) | copy-start | bytes 2654212
  2.8 20.6 %copy-start.1 = (bf16[16,16,384]{2,1,0:T(8,128)(2,1)S(1)}, bf16[16,16,384]{2,1,0:T(8,128)(2,1)}, u32[]{:S(2)}) copy-start(bf16[16,16,384]{2,1,0:T(8,128)(2,1)} %param.20) | copy-start | bytes 589828
  6.9 341.6 %all-to-all-start = ((bf16[32,2,1536]{2,1,0:T(2,128)(2,1)}), bf16[32,2,1536]{2,1,0:T(2,128)(2,1)S(1)}, u32[]{:S(2)}, u32[]{:S(2)}) async-start(bf16[32,2,1536]{2,1,0:T(2,128)(2,1)} %reshape.553), calls=%async_computation | async-start | bytes 393216 | tf_op jit(solution)/shard_map/all_to_all | solution.py:199
  23.4 314.1 %collective-permute-start = (bf16[2,16,384]{2,1,0:T(8,128)(2,1)S(1)}, bf16[2,16,384]{2,1,0:T(8,128)(2,1)S(1)}, u32[]{:S(2)}, u32[]{:S(2)}) collective-permute-start(bf16[2,16,384]{2,1,0:T(8,128)(2,1)S(1)} %get-tuple-element.637), channel_id=1, source_target_pairs={{0,32},{32,64},{64,96},{96,128},{128,160},{160,192},{192,224},{224... | collective-permute-start | bytes 73736 | tf_op jit(solution)/shard_map/ppermute | solution.py:22
  26.6 311.0 %collective-permute-start.1 = (bf16[2,16,384]{2,1,0:T(8,128)(2,1)S(1)}, bf16[2,16,384]{2,1,0:T(8,128)(2,1)S(1)}, u32[]{:S(2)}, u32[]{:S(2)}) collective-permute-start(bf16[2,16,384]{2,1,0:T(8,128)(2,1)S(1)} %get-tuple-element.636), channel_id=1, source_target_pairs={{32,0},{64,32},{96,64},{128,96},{160,128},{192,160},{224,192},{256... | collective-permute-start | bytes 73736 | tf_op jit(solution)/shard_map/ppermute | solution.py:24
  31.4 299.4 %copy-start.9 = (s32[16]{0:T(128)S(1)}, s32[16]{0:T(128)}, u32[]{:S(2)}) copy-start(s32[16]{0:T(128)} %param.24) | copy-start | bytes 196
  31.4 299.4 %copy-start.5 = (bf16[16,3,5,13]{3,0,2,1:T(8,128)(2,1)S(1)}, bf16[16,3,5,13]{3,0,2,1:T(8,128)(2,1)}, u32[]{:S(2)}) copy-start(bf16[16,3,5,13]{3,0,2,1:T(8,128)(2,1)} %param.22) | copy-start | bytes 18724
  338.3 28.2 %collective-permute-start.2 = (bf16[20,6,384]{2,1,0:T(8,128)(2,1)}, bf16[20,6,384]{2,1,0:T(8,128)(2,1)}, u32[]{:S(2)}, u32[]{:S(2)}) collective-permute-start(bf16[20,6,384]{2,1,0:T(8,128)(2,1)} %get-tuple-element.632), channel_id=1, source_target_pairs={{0,1},{1,2},{2,3},{3,4},{4,5},{5,6},{6,7},{7,8},{8,9},{9,10},{10,1... | collective-permute-start | bytes 276488 | tf_op jit(solution)/shard_map/ppermute | solution.py:22
  341.7 24.8 %collective-permute-start.3 = (bf16[20,6,384]{2,1,0:T(8,128)(2,1)}, bf16[20,6,384]{2,1,0:T(8,128)(2,1)}, u32[]{:S(2)}, u32[]{:S(2)}) collective-permute-start(bf16[20,6,384]{2,1,0:T(8,128)(2,1)} %get-tuple-element.633), channel_id=1, source_target_pairs={{1,0},{2,1},{3,2},{4,3},{5,4},{6,5},{7,6},{8,7},{9,8},{10,9},{11,1... | collective-permute-start | bytes 276488 | tf_op jit(solution)/shard_map/ppermute | solution.py:24
  349.6 5.8 copy-start.4
  359.2 13.6 %all-to-all-start.1 = ((bf16[16,2,2304]{2,1,0:T(2,128)(2,1)}), bf16[16,2,2304]{2,1,0:T(2,128)(2,1)S(1)}, u32[]{:S(2)}, u32[]{:S(2)}) async-start(bf16[16,2,2304]{2,1,0:T(2,128)(2,1)} %reshape.555), calls=%async_computation.1 | async-start | bytes 294912 | tf_op jit(solution)/shard_map/all_to_all | solution.py:204
  386.2 77.6 %copy-start.7 = (f32[192,12]{0,1:T(8,128)S(1)}, f32[192,12]{0,1:T(8,128)}, u32[]{:S(2)}) copy-start(f32[192,12]{0,1:T(8,128)} %param.21) | copy-start | bytes 27652
  495.1 10.5 %all-to-all-start.2 = ((bf16[16,2,2304]{2,1,0:T(2,128)(2,1)}), bf16[16,2,2304]{2,1,0:T(2,128)(2,1)S(1)}, u32[]{:S(2)}, u32[]{:S(2)}) async-start(bf16[16,2,2304]{2,1,0:T(2,128)(2,1)} %reshape.557), calls=%async_computation.2 | async-start | bytes 294912 | tf_op jit(solution)/shard_map/all_to_all | solution.py:214
  525.4 21.1 %all-to-all-start.3 = ((bf16[32,2,1536]{2,1,0:T(2,128)(2,1)}), bf16[32,2,1536]{2,1,0:T(2,128)(2,1)S(1)}, u32[]{:S(2)}, u32[]{:S(2)}) async-start(bf16[32,2,1536]{2,1,0:T(2,128)(2,1)} %reshape.559), calls=%async_computation.3 | async-start | bytes 393216 | tf_op jit(solution)/shard_map/all_to_all | solution.py:221
  559.8 4.8 copy-start.2
  559.8 4.8 copy-start.3
  564.6 22.1 %copy-start.6 = (bf16[16,3,5,13]{3,0,2,1:T(8,128)(2,1)S(1)}, bf16[16,3,5,13]{3,0,2,1:T(8,128)(2,1)}, u32[]{:S(2)}) copy-start(bf16[16,3,5,13]{3,0,2,1:T(8,128)(2,1)} %param.23) | copy-start | bytes 18724
  567.4 6.5 %collective-permute-start.4 = (bf16[2,16,384]{2,1,0:T(8,128)(2,1)S(1)}, bf16[2,16,384]{2,1,0:T(8,128)(2,1)S(1)}, u32[]{:S(2)}, u32[]{:S(2)}) collective-permute-start(bf16[2,16,384]{2,1,0:T(8,128)(2,1)S(1)} %get-tuple-element.634), channel_id=1, source_target_pairs={{0,32},{32,64},{64,96},{96,128},{128,160},{160,192},{192,224},{224... | collective-permute-start | bytes 73736 | tf_op jit(solution)/shard_map/ppermute | solution.py:22
  572.0 5.1 collective-permute-start.5
  577.2 12.3 %collective-permute-start.6 = (bf16[20,6,384]{2,1,0:T(8,128)(2,1)S(1)}, bf16[20,6,384]{2,1,0:T(8,128)(2,1)S(1)}, u32[]{:S(2)}, u32[]{:S(2)}) collective-permute-start(bf16[20,6,384]{2,1,0:T(8,128)(2,1)S(1)} %get-tuple-element.630), channel_id=1, source_target_pairs={{0,1},{1,2},{2,3},{3,4},{4,5},{5,6},{6,7},{7,8},{8,9},{9,10},{10,1... | collective-permute-start | bytes 276488 | tf_op jit(solution)/shard_map/ppermute | solution.py:22
  580.1 11.1 %collective-permute-start.7 = (bf16[20,6,384]{2,1,0:T(8,128)(2,1)S(1)}, bf16[20,6,384]{2,1,0:T(8,128)(2,1)S(1)}, u32[]{:S(2)}, u32[]{:S(2)}) collective-permute-start(bf16[20,6,384]{2,1,0:T(8,128)(2,1)S(1)} %get-tuple-element.631), channel_id=1, source_target_pairs={{1,0},{2,1},{3,2},{4,3},{5,4},{6,5},{7,6},{8,7},{9,8},{10,9},{11,1... | collective-permute-start | bytes 276488 | tf_op jit(solution)/shard_map/ppermute | solution.py:24
  595.3 2.9 copy-start.8
  595.3 3.1 copy-start.10
where the time goes:
time: 612 us; the launch traced here: 601 us
  local copies, waits for them, and re-layouts  158 us (26%)
  other arithmetic  149 us (24%)
  loops' own time  139 us (23%)
  starting transfers between devices  68.5 us (11%)
  matrix products  59.8 us (10%)
  waiting for transfers between devices  26.4 us (4%)
    another operation x1, loops' own time, legendre_table(): lax.scan(advance, (zero_field, zero_field), jnp.arange(degrees, dtype=jnp...  124 us
    lt x24, other arithmetic, advance(): entry = jnp.where(degree < orders[None, :], jnp.zeros_like(entry), entry)  119 us
    dynamic_update_slice x24, local copies, waits for them, and re-layouts, forward_advance_block(): return lax.dynamic_update_slice_in_dim(running, portion, degree_start, 3)  41.2 us
    dot_general x12, matrix products, forward_compute(): jnp.einsum('cqgi,lig->cqgl', spectra_in, plm_block, precision=lax.Precisi...  29 us
    unnamed x42, local copies, waits for them, and re-layouts  28.8 us
    dot_general x12, matrix products, inverse_compute(): jnp.einsum('cqgl,lig->cqgi', portion, plm_block, precision=lax.Precision....  18.4 us
    ppermute x4, starting transfers between devices, extended_2(): lax.ppermute(head, axis, [((i + 1) % count, i) for i in range(ends)])  17.2 us
    all_to_all x1, starting transfers between devices, local(): lax.all_to_all(turned, 'lon', split_axis=1, concat_axis=2, tiled=True)  16.5 us
  transfers between devices with their start and end apart: 12, of which 6 were waited for; matrix products, arithmetic and copies ran while one was open for 34% of the time, Pallas kernels for 0%

commit v1 on v0

v1 whole, which is shorter than its diff:
```python
import functools
import math

import jax
import jax.numpy as jnp
from jax import lax
from jax.experimental import pallas as pl
from jax.experimental.pallas import tpu as pltpu
from jax.sharding import PartitionSpec as P

C = 384
CL = 12
CP = 16
KB = 3
RLAT = 2
RLON = 6
TAPS = 2 * RLON + 1
DLAT = 2 * RLAT + 1
NLAT = 256
NLON = 512
PLAT = 16
PLON = 32
A = 16
N = 16
M = 192
ML = 12
AX = A + 2 * RLAT
JX = 32
OFF = 8
F32 = jnp.float32
BF = jnp.bfloat16
NT = (((1,), (1,)), ((), ()))
VMEM_LIMIT = 48 * 1024 * 1024


def call(kernel, outs, scratch, *args, smem=(), flops=1_000_000, moved=1_000_000):
    specs = [
        pl.BlockSpec(memory_space=pltpu.SMEM if i in smem else pltpu.VMEM)
        for i in range(len(args))
    ]
    out_specs = jax.tree.map(lambda _: pl.BlockSpec(memory_space=pltpu.VMEM), outs)
    return pl.pallas_call(
        kernel,
        out_shape=outs,
        in_specs=specs,
        out_specs=out_specs,
        scratch_shapes=scratch,
        cost_estimate=pl.CostEstimate(flops=flops, bytes_accessed=moved, transcendentals=0),
        compiler_params=pltpu.CompilerParams(vmem_limit_bytes=VMEM_LIMIT),
    )(*args)


def swap_blocks(pieces, width):
    count = len(pieces)
    pieces = list(pieces)
    block = lax.broadcasted_iota(jnp.int32, pieces[0].shape, 1) // width
    step = 1
    while step < count:
        low = (block & step) == 0
        for i in range(count):
            if i & step:
                continue
            x, y = pieces[i], pieces[i | step]
            pieces[i] = jnp.where(low, x, pltpu.roll(y, step * width, 1))
            pieces[i | step] = jnp.where(low, pltpu.roll(x, 128 - step * width, 1), y)
        step *= 2
    return pieces


def prep_kernel(fields_ref, out_ref, rows):
    turned = fields_ref[...].reshape(A * N, C).astype(F32).T
    for hi in range(2):
        rows[pl.ds(hi, C, stride=2), :] = turned[:, hi * 128 : hi * 128 + 128]
    for d in range(PLON):
        out_ref[d] = rows[24 * d : 24 * d + 24, :].astype(BF)


def table_kernel(order_ref, cos_ref, diag_ref, out_ref, rows):
    order = order_ref[...]
    square = order * order
    cosine = [jnp.broadcast_to(cos_ref[:, h * 128 : h * 128 + 128], (CP, 128)) for h in range(2)]
    diag = [diag_ref[:, h * 128 : h * 128 + 128] for h in range(2)]
    zero = order * 0.0

    def step(degree, state):
        deg = jnp.full((CP, 128), degree, jnp.int32).astype(F32)
        back = deg - 1.0
        up = jnp.sqrt(jnp.maximum(4.0 * deg * deg - 1.0, 0.0) / jnp.maximum(deg * deg - square, 1.0))
        down = jnp.sqrt(
            jnp.maximum(back * back - square, 0.0) / jnp.maximum(4.0 * back * back - 1.0, 1.0)
        )
        new = []
        for h in range(2):
            previous, earlier = state[2 * h], state[2 * h + 1]
            entry = (up * cosine[h]) * previous - (up * down) * earlier
            entry = jnp.where(order == deg, diag[h], entry)
            rows[h, pl.ds(pl.multiple_of(degree * CP, CP), CP), :] = entry
            new += [entry, previous]
        return tuple(new)

    lax.fori_loop(0, M, step, (zero,) * 4, unroll=8)
    for m in range(ML):
        for h in range(2):
            out_ref[m, :, h * 128 : h * 128 + 128] = rows.at[h][
                pl.ds(m, M, stride=CP), :
            ].astype(BF)


def forward_kernel(recv_ref, u_ref, v_ref, c_ref, s_ref, out_ref, grid, rows):
    pieces = [
        jnp.concatenate([recv_ref[hi * 8 + lo].astype(F32) for hi in range(4)], axis=0)
        for lo in range(8)
    ]
    pieces = swap_blocks(pieces, 16)
    for hi in range(4):
        for lo in range(8):
            grid.at[hi][pl.ds(lo, 24, stride=8), :] = pieces[lo][hi * 24 : hi * 24 + 24]
        grid[hi, 192:256, :] = jnp.zeros((64, 128), F32)
    circles = jnp.concatenate([grid[hi].astype(BF) for hi in range(4)], axis=1)
    cosb, sinb = c_ref[...], s_ref[...]
    table = jnp.concatenate(
        [
            (u_ref[s : s + 1, :] * cosb + v_ref[s : s + 1, :] * sinb).astype(BF)
            for s in range(PLON)
        ],
        axis=0,
    )
    spectra = jnp.dot(circles, table, preferred_element_type=F32).T
    for g in range(2):
        rows[pl.ds(g, 2 * M, stride=2), :] = spectra[:, g * 128 : g * 128 + 128]
    for e in range(PLAT):
        out_ref[e] = rows[48 * e : 48 * e + 48, :].astype(BF)


def split(value):
    high = value.astype(BF)
    low = (value - high.astype(F32)).astype(BF)
    return jnp.concatenate([high, low], axis=0)


def legendre_kernel(recv_ref, tab_ref, quad_ref, gain_ref, out_ref, grid, res):
    pieces = [
        jnp.concatenate([recv_ref[hi * 8 + lo].astype(F32) for hi in range(2)], axis=0)
        for lo in range(8)
    ]
    pieces = swap_blocks(pieces, 16)
    for hi in range(2):
        for x in range(8):
            grid.at[hi][pl.ds(x, 48, stride=8), :] = pieces[x][hi * 48 : hi * 48 + 48]
    gain = gain_ref[...]
    quad = quad_ref[...]
    for m in range(ML):
        part = slice(32 * m, 32 * m + 32)
        weighted = jnp.concatenate([grid[0, part, :], grid[1, part, :]], axis=1) * quad
        table = tab_ref[m]
        both = lax.dot_general(split(weighted), table, NT, preferred_element_type=F32)
        harmonics = (both[:32] + both[32:]) * gain
        both = jnp.dot(split(harmonics), table, preferred_element_type=F32)
        result = both[:32] + both[32:]
        for r in range(2):
            at = (2 * m + r) * CL
            for h in range(2):
                res[h, at : at + CL, :] = result[16 * r : 16 * r + CL, h * 128 : h * 128 + 128]
    lanes = lax.broadcasted_iota(jnp.int32, (72, 128), 1)
    place = lanes // 32
    inner = lanes % 32
    source = [[res.at[h][pl.ds(lo, 72, stride=4), :] for lo in range(4)] for h in range(2)]
    for j in range(PLAT):
        total = None
        for lo in range(4):
            shift = (lo * 32 - (16 * j - RLAT)) % 128
            value = pltpu.roll(source[j // 8][lo], shift, 1) if shift else source[j // 8][lo]
            if j in (7, 8):
                other = source[1 - j // 8][lo]
                other = pltpu.roll(other, shift, 1) if shift else other
                bound = 128 - (16 * 7 - RLAT) if j == 7 else RLAT
                first, last = (value, other) if j == 7 else (other, value)
                value = jnp.where(inner < bound, first, last)
            total = value if total is None else jnp.where(place == lo, value, total)
        out_ref[j] = total.astype(BF)


def inverse_kernel(recv_ref, u_ref, v_ref, c_ref, s_ref, out_ref, rows, coef, grid):
    for e in range(PLAT):
        rows[72 * e : 72 * e + 72, :] = recv_ref[e].astype(F32)
    for hi in range(3):
        turned = rows[pl.ds(hi, 2 * M, stride=3), :].T
        for lo in range(4):
            at = (hi * 4 + lo) * AX
            coef[at : at + AX, :] = turned[lo * 32 : lo * 32 + AX, :]
    left = coef[...].astype(BF)
    cosb, sinb = c_ref[...], s_ref[...]
    for k in range(8):
        table = jnp.concatenate(
            [
                (u_ref[d : d + 1, :] * cosb + v_ref[d : d + 1, :] * sinb).astype(BF)
                for d in range(4 * k, 4 * k + 4)
            ],
            axis=0,
        )
        grid[k] = lax.dot_general(left, table, NT, preferred_element_type=F32)
    for k in range(8):
        pieces = [grid.at[k][pl.ds(lo, 60, stride=4), :] for lo in range(4)]
        pieces = swap_blocks(pieces, 32)
        for lo in range(4):
            out_ref[4 * k + lo] = pieces[lo].astype(BF)


def gather_rows(taps_ref, field, mixing_ref, gathered, rows, cols, wide, start):
    lanes = taps_ref.shape[1]
    for a in range(rows):
        bands = []
        for k in range(KB):
            line = taps_ref[a * KB + k : a * KB + k + 1, :]
            band = pltpu.roll(
                jnp.broadcast_to(line, (cols, lanes)), start, 1, stride=1, stride_axis=0
            )
            bands.append(band.astype(BF))
        band = jnp.concatenate(bands, axis=0)[:, : DLAT * wide]
        value = jnp.dot(
            band, field[a * wide : (a + DLAT) * wide, :], preferred_element_type=F32
        ).astype(BF)
        for k in range(KB):
            gathered[k, a * cols : (a + 1) * cols, :] = value[k * cols : (k + 1) * cols]
    total = jnp.dot(gathered[0], mixing_ref[0], preferred_element_type=F32)
    for k in range(1, KB):
        total += jnp.dot(gathered[k], mixing_ref[k], preferred_element_type=F32)
    return total


def first_kernel(rim_ref, left_ref, right_ref, taps_ref, mix_ref, out_ref, field, gathered):
    for a in range(AX + 2 * RLAT):
        field[48 * a : 48 * a + 16, :] = left_ref[a]
        field[48 * a + 16 : 48 * a + 32, :] = rim_ref[a]
        field[48 * a + 32 : 48 * a + 48, :] = right_ref[a]
    first = gather_rows(taps_ref, field, mix_ref, gathered, AX, JX, 48, 16 - OFF - RLON)
    for a in range(AX):
        at = (a + RLAT) * 48 + 16 - OFF
        own = field[(a + RLAT) * 48 : (a + RLAT) * 48 + 48, :].astype(F32)
        out_ref[a * JX : (a + 1) * JX, :] = (
            first[a * JX : (a + 1) * JX] + own[16 - OFF : 16 - OFF + JX]
        )


def last_kernel(
    place_ref, recv_ref, pre_ref, taps_ref, mix_ref, norm_ref, in_ref, back_ref, out_ref,
    rows, stream, exact, gathered,
):
    place = place_ref[0]
    for s in range(PLON):
        rows[60 * s : 60 * s + 60, :] = recv_ref[s].astype(F32)
    for hi in range(5):
        spectral = rows[pl.ds(hi, C, stride=5), :].T
        value = pre_ref[128 * hi : 128 * hi + 128, :] + spectral
        row = lax.broadcasted_iota(jnp.int32, (128, C), 0) // JX + 4 * hi - RLAT + place * A
        value = jnp.where((row >= 0) & (row < NLAT), value, 0.0).astype(BF)
        stream[128 * hi : 128 * hi + 128, :] = value
        exact[128 * hi : 128 * hi + 128, :] = value.astype(F32)
    second = gather_rows(taps_ref, stream, mix_ref, gathered, A, N, JX, OFF - RLON)
    own = jnp.concatenate(
        [exact[(a + RLAT) * JX + OFF : (a + RLAT) * JX + OFF + N, :] for a in range(A)], axis=0
    )
    summed = own + second
    center = summed - jnp.mean(summed, axis=-1, keepdims=True)
    spread = jnp.mean(center * center, axis=-1, keepdims=True)
    normed = (center * lax.rsqrt(spread + 1e-05) * norm_ref[...]).astype(BF)
    hidden = jax.nn.gelu(jnp.dot(normed, in_ref[...], preferred_element_type=F32)).astype(BF)
    update = jnp.dot(hidden, back_ref[...], preferred_element_type=F32)
    out_ref[...] = (own + update).astype(BF).reshape(A, N, C)


def circle(product):
    return 2.0 * math.pi / NLON * (product % NLON).astype(F32)


def sector_tables(cells, doubled):
    orders = jnp.arange(M, dtype=jnp.int32)
    sectors = N * jnp.arange(PLON, dtype=jnp.int32)
    outer = circle(sectors[:, None] * orders[None, :])
    inner = circle(cells[:, None] * orders[None, :])
    scale = jnp.where(orders == 0, 1.0, 2.0).astype(F32) if doubled else 1.0
    cos, sin = jnp.cos(outer) * scale, jnp.sin(outer) * scale
    u = jnp.stack([cos, -sin], axis=-1).reshape(PLON, 2 * M)
    v = jnp.stack([-sin, -cos], axis=-1).reshape(PLON, 2 * M)
    return u, v, jnp.repeat(jnp.cos(inner), 2, axis=1), jnp.repeat(jnp.sin(inner), 2, axis=1)


def legendre_start(colatitude, orders, degrees):
    order_vals = orders.astype(F32)
    counter = jnp.arange(1, degrees + 1, dtype=jnp.int32).astype(F32)
    factors = jnp.log((2.0 * counter - 1.0) / (2.0 * counter))
    partial_sum = jnp.sum(
        jnp.where(counter[None, :] <= order_vals[:, None], factors[None, :], 0.0), axis=1
    )
    log_sine = jnp.log(jnp.sin(colatitude))
    start_log = 0.5 * jnp.log((2.0 * order_vals + 1.0) / (4.0 * math.pi)) + 0.5 * partial_sum
    return jnp.exp(start_log[:, None] + order_vals[:, None] * log_sine[None, :])


def shifted(value, axis, by, closed):
    count = lax.axis_size(axis)
    pairs = [(i, (i + by) % count) for i in range(count) if closed or 0 <= i + by < count]
    return lax.ppermute(value, axis, pairs)


def tap_lines(stencil, cycle_reach, wide, lanes):
    rows = stencil.shape[0]
    offsets = jnp.arange(TAPS, dtype=jnp.int32) - RLON
    inside = (jnp.abs(offsets)[None, :] <= cycle_reach[:, None]).astype(BF)
    masked = stencil * inside[:, None, None, :]
    masked = jnp.pad(masked, ((0, 0), (0, 0), (0, 0), (0, wide - TAPS)))
    masked = masked.reshape(rows, KB, DLAT * wide)
    return jnp.pad(masked, ((0, 0), (0, 0), (0, lanes - DLAT * wide)))


def exchange(block, axis):
    return lax.all_to_all(block, axis, split_axis=0, concat_axis=0, tiled=True)


def shape(dims, dtype):
    return jax.ShapeDtypeStruct(dims, dtype)


def local(
    fields, spectral_gain, stencil_one, stencil_two, cycle_reach, mix_one, mix_two, norm_gain,
    w_in, w_out,
):
    place = lax.axis_index("lat")
    colatitude = math.pi * (jnp.arange(NLAT, dtype=jnp.int32).astype(F32) + 0.5) / NLAT
    quad = math.pi / NLAT * (2.0 * math.pi / NLON) * jnp.sin(colatitude)
    own_orders = place * ML + jnp.minimum(jnp.arange(CP, dtype=jnp.int32), ML - 1)
    diagonal = legendre_start(colatitude, own_orders, M)

    sent = call(
        prep_kernel, shape((PLON, 24, 128), BF), [pltpu.VMEM((768, 128), F32)], fields
    )
    recv = exchange(sent, "lon")

    lines_one = tap_lines(stencil_one, cycle_reach, 48, 256)
    lines_two = tap_lines(stencil_two, cycle_reach, JX, 256).reshape(A * KB, 256).astype(F32)
    edge = 2 * RLAT

    def packed(cells, lines):
        extra = jnp.pad(lines.reshape(1, 4, C), ((0, 0), (0, N - 4), (0, 0)))
        return jnp.concatenate([cells, extra], axis=0)

    above = shifted(packed(fields[A - edge :], lines_one[A - RLAT :]), "lat", 1, False)
    below = shifted(packed(fields[:edge], lines_one[:RLAT]), "lat", -1, False)
    rim = jnp.concatenate([above[:edge], fields, below[:edge]], axis=0)
    taps_one = (
        jnp.concatenate(
            [
                above[edge, :4].reshape(RLAT, KB, 256),
                lines_one,
                below[edge, :4].reshape(RLAT, KB, 256),
            ],
            axis=0,
        )
        .reshape(AX * KB, 256)
        .astype(F32)
    )
    left = shifted(rim, "lon", 1, True)
    right = shifted(rim, "lon", -1, True)

    table = call(
        table_kernel,
        shape((ML, M, NLAT), BF),
        [pltpu.VMEM((2, M * CP, 128), F32)],
        jnp.broadcast_to(own_orders.astype(F32)[:, None], (CP, 128)),
        jnp.cos(colatitude)[None, :],
        diagonal,
    )
    spectra = call(
        forward_kernel,
        shape((PLAT, 48, 128), BF),
        [pltpu.VMEM((4, 256, 128), F32), pltpu.VMEM((768, 128), F32)],
        recv,
        *sector_tables(jnp.arange(N, dtype=jnp.int32), False),
    )
    gathered = exchange(spectra, "lat")
    gain = jnp.pad(spectral_gain.T, ((0, CP - CL), (0, 0)))
    results = call(
        legendre_kernel,
        shape((PLAT, 72, 128), BF),
        [pltpu.VMEM((2, 384, 128), F32), pltpu.VMEM((2, 288, 128), F32)],
        gathered,
        table,
        quad[None, :],
        jnp.concatenate([gain, gain], axis=0),
    )
    returned = exchange(results, "lat")
    sectors = call(
        inverse_kernel,
        shape((PLON, 60, 128), BF),
        [
            pltpu.VMEM((1152, 128), F32),
            pltpu.VMEM((CL * AX, 2 * M), F32),
            pltpu.VMEM((8, CL * AX, 128), F32),
        ],
        returned,
        *sector_tables(jnp.arange(JX, dtype=jnp.int32) - OFF, True),
    )
    spectral = exchange(sectors, "lon")
    pre = call(
        first_kernel,
        shape((AX * JX, C), F32),
        [pltpu.VMEM(((AX + edge) * 48, C), BF), pltpu.VMEM((KB, AX * JX, C), BF)],
        rim,
        left,
        right,
        taps_one,
        mix_one,
    )
    return call(
        last_kernel,
        shape((A, N, C), BF),
        [
            pltpu.VMEM((1920, 128), F32),
            pltpu.VMEM((AX * JX, C), BF),
            pltpu.VMEM((AX * JX, C), F32),
            pltpu.VMEM((KB, A * N, C), BF),
        ],
        place.reshape(1),
        spectral,
        pre,
        lines_two,
        mix_two,
        norm_gain[None, :],
        w_in,
        w_out,
        smem=(0,),
    )


def solution(mesh):
    in_specs = (
        P("lat", "lon", None),
        P(None, "lon"),
        P("lat", None, None, None),
        P("lat", None, None, None),
        P("lat"),
        P(),
        P(),
        P(),
        P(),
        P(),
    )
    out_specs = P("lat", "lon", None)
    return jax.shard_map(local, mesh=mesh, in_specs=in_specs, out_specs=out_specs, check_vma=False)
```

time: 612 us -> 111 us (0.18)
  the two profiles are of different devices: /device:TPU:1 before, /device:TPU:2 now
where the time goes in v1:
time: 111 us; the launch traced here: 110 us
  starting transfers between devices  47.7 us (43%)
  waiting for transfers between devices  36 us (32%)
  Pallas kernels  15.2 us (14%)
  local copies, waits for them, and re-layouts  8.92 us (8%)
  other arithmetic  2.07 us (2%)
    all_to_all x4, starting transfers between devices, exchange(): return lax.all_to_all(block, axis, split_axis=0, concat_axis=0, tiled=True)  30.9 us
    ppermute x4, waiting for transfers between devices, shifted(): return lax.ppermute(value, axis, pairs)  19.2 us
    ppermute x4, starting transfers between devices, shifted(): return lax.ppermute(value, axis, pairs)  16.8 us
    all_to_all x4, waiting for transfers between devices, exchange(): return lax.all_to_all(block, axis, split_axis=0, concat_axis=0, tiled=True)  16.8 us
    pallas_call x7, Pallas kernels, call(): pl.pallas_call(kernel, out_shape=outs, in_specs=specs, out_specs=out_spec...  15.2 us
    unnamed x32, local copies, waits for them, and re-layouts  6.62 us
  transfers between devices with their start and end apart: 8, of which 6 were waited for; matrix products, arithmetic and copies ran while one was open for 4% of the time, Pallas kernels for 5%

profile of v1, /device:TPU:2, one launch (start us, length us, event | category | flops | bytes accessed | tf_op | source)
XLA Modules:
  0.0 110.4 jit_solution(4295304775195818012)
XLA Ops:
  0.0 0.9 copy-done
  0.9 0.8 shard_map.100
  1.8 16.0 %all-to-all-start = ((bf16[32,24,128]{2,1,0:T(8,128)(2,1)}), bf16[32,24,128]{2,1,0:T(8,128)(2,1)S(1)}, u32[]{:S(2)}, u32[]{:S(2)}) async-start(bf16[32,24,128]{2,1,0:T(8,128)(2,1)} %shard_map.100), calls=%async_computation | async-start | bytes 393216 | tf_op jit(solution)/shard_map/all_to_all | solution.py:317
  17.8 0.4 fusion.19
  18.2 0.4 fusion.18
  18.8 0.2 fusion.30
  20.0 0.4 fusion.16
  20.4 10.7 %all-to-all-done.recv_ref = bf16[32,24,128]{2,1,0:T(8,128)(2,1)S(1)} async-done(((bf16[32,24,128]{2,1,0:T(8,128)(2,1)}), bf16[32,24,128]{2,1,0:T(8,128)(2,1)S(1)}, u32[]{:S(2)}, u32[]{:S(2)}) %all-to-all-start) | async-done | bytes 196640 | tf_op jit(solution)/shard_map/all_to_all | solution.py:317
  31.1 1.4 %shard_map.101 = bf16[16,48,128]{2,1,0:T(8,128)(2,1)} custom-call(bf16[32,24,128]{2,1,0:T(8,128)(2,1)S(1)} %all-to-all-done.recv_ref, f32[32,384]{1,0:T(8,128)S(1)} %copy.49.u_ref, f32[32,384]{1,0:T(8,128)S(1)} %copy.50.v_ref, f32[16,384]{1,0:T(8,128)S(1)} %copy.51.c_ref, f32[16,384]{1,0:T(8,128)S(1)} %copy.52.s_ref), custom_call_target="tpu_custom_call" | custom-call | flops 1000000 | bytes 1000000 | tf_op jit(solution)/shard_map/pallas_call | solution.py:42
  32.5 5.2 %all-to-all-start.1 = ((bf16[16,48,128]{2,1,0:T(8,128)(2,1)}), bf16[16,48,128]{2,1,0:T(8,128)(2,1)S(1)}, u32[]{:S(2)}, u32[]{:S(2)}) async-start(bf16[16,48,128]{2,1,0:T(8,128)(2,1)} %shard_map.101), calls=%async_computation.1 | async-start | bytes 393216 | tf_op jit(solution)/shard_map/all_to_all | solution.py:317
  38.8 3.2 %shard_map.102.tab_ref = bf16[12,192,256]{2,1,0:T(8,128)(2,1)S(1)} custom-call(f32[16,128]{1,0:T(8,128)S(1)} %broadcast_in_dim.28.order_ref, f32[1,256]{1,0:T(1,128)S(1)} %fusion.32.cos_ref, f32[16,256]{1,0:T(8,128)S(1)} %add_exponential_fusion.diag_ref), custom_call_target="tpu_custom_call" | custom-call | flops 1000000 | bytes 1000000 | tf_op jit(solution)/shard_map/pallas_call | solution.py:42
  42.2 0.6 all-to-all-done.1.recv_ref
  42.7 3.3 %shard_map.103 = bf16[16,72,128]{2,1,0:T(8,128)(2,1)} custom-call(bf16[16,48,128]{2,1,0:T(8,128)(2,1)S(1)} %all-to-all-done.1.recv_ref, bf16[12,192,256]{2,1,0:T(8,128)(2,1)S(1)} %shard_map.102.tab_ref, f32[1,256]{1,0:T(1,128)S(1)} %sine_multiply_fusion.quad_ref, f32[32,192]{1,0:T(8,128)S(1)} %pad_maximum_fusion.5.gain_ref), custom_call_target="tpu_custom_call" | custom-call | flops 1000000 | bytes 1000000 | tf_op jit(solution)/shard_map/pallas_call | solution.py:42
  46.1 5.8 %all-to-all-start.2 = ((bf16[16,72,128]{2,1,0:T(8,128)(2,1)}), bf16[16,72,128]{2,1,0:T(8,128)(2,1)S(1)}, u32[]{:S(2)}, u32[]{:S(2)}) async-start(bf16[16,72,128]{2,1,0:T(8,128)(2,1)} %shard_map.103), calls=%async_computation.2 | async-start | bytes 589824 | tf_op jit(solution)/shard_map/all_to_all | solution.py:317
  52.2 5.5 %all-to-all-done.2.recv_ref = bf16[16,72,128]{2,1,0:T(8,128)(2,1)S(1)} async-done(((bf16[16,72,128]{2,1,0:T(8,128)(2,1)}), bf16[16,72,128]{2,1,0:T(8,128)(2,1)S(1)}, u32[]{:S(2)}, u32[]{:S(2)}) %all-to-all-start.2) | async-done | bytes 294944 | tf_op jit(solution)/shard_map/all_to_all | solution.py:317
  57.7 1.8 %shard_map.104 = bf16[32,60,128]{2,1,0:T(8,128)(2,1)} custom-call(bf16[16,72,128]{2,1,0:T(8,128)(2,1)S(1)} %all-to-all-done.2.recv_ref, f32[32,384]{1,0:T(8,128)S(1)} %copy.55.u_ref, f32[32,384]{1,0:T(8,128)S(1)} %copy.56.v_ref, f32[32,384]{1,0:T(8,128)S(1)} %copy.57.c_ref, f32[32,384]{1,0:T(8,128)S(1)} %copy.58.s_ref), custom_call_target="tpu_custom_call" | custom-call | flops 1000000 | bytes 1000000 | tf_op jit(solution)/shard_map/pallas_call | solution.py:42
  59.5 3.9 %all-to-all-start.3 = ((bf16[32,60,128]{2,1,0:T(8,128)(2,1)}), bf16[32,60,128]{2,1,0:T(8,128)(2,1)S(1)}, u32[]{:S(2)}, u32[]{:S(2)}) async-start(bf16[32,60,128]{2,1,0:T(8,128)(2,1)} %shard_map.104), calls=%async_computation.3 | async-start | bytes 1048576 | tf_op jit(solution)/shard_map/all_to_all | solution.py:317
  63.5 2.7 %collective-permute-start = (bf16[5,16,384]{2,1,0:T(8,128)(2,1)S(1)}, bf16[5,16,384]{2,1,0:T(8,128)(2,1)S(1)}, u32[]{:S(2)}, u32[]{:S(2)}) collective-permute-start(bf16[5,16,384]{2,1,0:T(8,128)(2,1)S(1)} %fusion.14), channel_id=1, source_target_pairs={{0,32},{32,64},{64,96},{96,128},{128,160},{160,192},{192,224},{224... | collective-permute-start | bytes 184328 | tf_op jit(solution)/shard_map/ppermute | solution.py:303
  66.3 3.9 %collective-permute-start.1 = (bf16[5,16,384]{2,1,0:T(8,128)(2,1)S(1)}, bf16[5,16,384]{2,1,0:T(8,128)(2,1)S(1)}, u32[]{:S(2)}, u32[]{:S(2)}) collective-permute-start(bf16[5,16,384]{2,1,0:T(8,128)(2,1)S(1)} %fusion.15), channel_id=1, source_target_pairs={{32,0},{64,32},{96,64},{128,96},{160,128},{192,160},{224,192},{256... | collective-permute-start | bytes 184328 | tf_op jit(solution)/shard_map/ppermute | solution.py:303
  70.2 8.8 %collective-permute-done = bf16[5,16,384]{2,1,0:T(8,128)(2,1)S(1)} collective-permute-done((bf16[5,16,384]{2,1,0:T(8,128)(2,1)S(1)}, bf16[5,16,384]{2,1,0:T(8,128)(2,1)S(1)}, u32[]{:S(2)}, u32[]{:S(2)}) %collective-permute-start) | collective-permute-done | bytes 61472 | tf_op jit(solution)/shard_map/ppermute | solution.py:303
  79.0 3.0 %collective-permute-start.2 = (bf16[24,16,384]{2,1,0:T(8,128)(2,1)S(1)}, bf16[24,16,384]{2,1,0:T(8,128)(2,1)S(1)}, u32[]{:S(2)}, u32[]{:S(2)}) collective-permute-start(bf16[24,16,384]{2,1,0:T(8,128)(2,1)S(1)} %pad_maximum_fusion.rim_ref), channel_id=1, source_target_pairs={{0,1},{1,2},{2,3},{3,4},{4,5},{5,6},{6,7},{7,8},{8,9},{9,10},{10,1... | collective-permute-start | bytes 884744 | tf_op jit(solution)/shard_map/ppermute | solution.py:303
  82.0 7.3 %collective-permute-start.3 = (bf16[24,16,384]{2,1,0:T(8,128)(2,1)S(1)}, bf16[24,16,384]{2,1,0:T(8,128)(2,1)S(1)}, u32[]{:S(2)}, u32[]{:S(2)}) collective-permute-start(bf16[24,16,384]{2,1,0:T(8,128)(2,1)S(1)} %pad_maximum_fusion.rim_ref), channel_id=1, source_target_pairs={{0,31},{1,0},{2,1},{3,2},{4,3},{5,4},{6,5},{7,6},{8,7},{9,8},{10,9... | collective-permute-start | bytes 884744 | tf_op jit(solution)/shard_map/ppermute | solution.py:303
  89.8 4.1 %collective-permute-done.2.left_ref = bf16[24,16,384]{2,1,0:T(8,128)(2,1)S(1)} collective-permute-done((bf16[24,16,384]{2,1,0:T(8,128)(2,1)S(1)}, bf16[24,16,384]{2,1,0:T(8,128)(2,1)S(1)}, u32[]{:S(2)}, u32[]{:S(2)}) %collective-permute-start.2) | collective-permute-done | bytes 294944 | tf_op jit(solution)/shard_map/ppermute | solution.py:303
  93.9 0.7 copy-done.6
  94.6 6.3 %collective-permute-done.3.right_ref = bf16[24,16,384]{2,1,0:T(8,128)(2,1)S(1)} collective-permute-done((bf16[24,16,384]{2,1,0:T(8,128)(2,1)S(1)}, bf16[24,16,384]{2,1,0:T(8,128)(2,1)S(1)}, u32[]{:S(2)}, u32[]{:S(2)}) %collective-permute-start.3) | collective-permute-done | bytes 294944 | tf_op jit(solution)/shard_map/ppermute | solution.py:303
  100.9 0.7 copy-done.8
  101.6 1.0 copy-done.7
  102.6 1.0 copy-done.9
  103.6 1.9 %shard_map.105.pre_ref = f32[640,384]{1,0:T(8,128)S(1)} custom-call(bf16[24,16,384]{2,1,0:T(8,128)(2,1)S(1)} %pad_maximum_fusion.rim_ref, bf16[24,16,384]{2,1,0:T(8,128)(2,1)S(1)} %copy-done.7, bf16[24,16,384]{2,1,0:T(8,128)(2,1)S(1)} %copy-done.9, f32[60,256]{1,0:T(8,128)S(1)} %reshape.423.taps_ref, bf16[3,384,384]{2,1,0:T(8,128)(2,1)S(1)} %copy-done.2), custom_call_target="tpu_custom_call" | custom-call | flops 1000000 | bytes 1000000 | tf_op jit(solution)/shard_map/pallas_call | solution.py:42
  105.5 1.2 %copy-done.3 = bf16[3,384,384]{2,1,0:T(8,128)(2,1)S(1)} copy-done((bf16[3,384,384]{2,1,0:T(8,128)(2,1)S(1)}, bf16[3,384,384]{2,1,0:T(8,128)(2,1)}, u32[]{:S(2)}) %copy-start.3) | copy-done | bytes 884760
  106.7 1.1 copy-done.5
  107.7 2.7 %shard_map.106 = bf16[16,16,384]{2,1,0:T(8,128)(2,1)} custom-call(s32[1]{0:T(128)} %bitcast.place_ref, bf16[32,60,128]{2,1,0:T(8,128)(2,1)S(1)} %all-to-all-done.3.recv_ref, f32[640,384]{1,0:T(8,128)S(1)} %shard_map.105.pre_ref, f32[48,256]{1,0:T(8,128)S(1)} %reshape.424.taps_ref, bf16[3,384,384]{2,1,0:T(8,128)(2,1)S(1)} %copy-done.3, ...), custom_call_target="tpu_custom_call" | custom-call | flops 1000000 | bytes 1000000 | tf_op jit(solution)/shard_map/pallas_call | solution.py:42
  (91 shorter events, 3.1 us)
Async XLA Ops:
  0.0 0.9 copy-start
  1.8 29.3 %all-to-all-start = ((bf16[32,24,128]{2,1,0:T(8,128)(2,1)}), bf16[32,24,128]{2,1,0:T(8,128)(2,1)S(1)}, u32[]{:S(2)}, u32[]{:S(2)}) async-start(bf16[32,24,128]{2,1,0:T(8,128)(2,1)} %shard_map.100), calls=%async_computation | async-start | bytes 393216 | tf_op jit(solution)/shard_map/all_to_all | solution.py:317
  32.5 6.1 %copy-start.12 = (f32[192,12]{0,1:T(8,128)S(1)}, f32[192,12]{0,1:T(8,128)}, u32[]{:S(2)}) copy-start(f32[192,12]{0,1:T(8,128)} %param.11) | copy-start | bytes 27652
  32.5 10.2 %all-to-all-start.1 = ((bf16[16,48,128]{2,1,0:T(8,128)(2,1)}), bf16[16,48,128]{2,1,0:T(8,128)(2,1)S(1)}, u32[]{:S(2)}, u32[]{:S(2)}) async-start(bf16[16,48,128]{2,1,0:T(8,128)(2,1)} %shard_map.101), calls=%async_computation.1 | async-start | bytes 393216 | tf_op jit(solution)/shard_map/all_to_all | solution.py:317
  42.1 9.8 %copy-start.14 = (s32[16]{0:T(128)S(1)}, s32[16]{0:T(128)}, u32[]{:S(2)}) copy-start(s32[16]{0:T(128)} %param.14) | copy-start | bytes 196
  42.1 9.9 %copy-start.10 = (bf16[16,3,5,13]{3,0,2,1:T(8,128)(2,1)S(1)}, bf16[16,3,5,13]{3,0,2,1:T(8,128)(2,1)}, u32[]{:S(2)}) copy-start(bf16[16,3,5,13]{3,0,2,1:T(8,128)(2,1)} %param.13) | copy-start | bytes 18724
  42.1 9.9 %copy-start.11 = (bf16[16,3,5,13]{3,0,2,1:T(8,128)(2,1)S(1)}, bf16[16,3,5,13]{3,0,2,1:T(8,128)(2,1)}, u32[]{:S(2)}) copy-start(bf16[16,3,5,13]{3,0,2,1:T(8,128)(2,1)} %param.12) | copy-start | bytes 18724
  46.1 11.6 %all-to-all-start.2 = ((bf16[16,72,128]{2,1,0:T(8,128)(2,1)}), bf16[16,72,128]{2,1,0:T(8,128)(2,1)S(1)}, u32[]{:S(2)}, u32[]{:S(2)}) async-start(bf16[16,72,128]{2,1,0:T(8,128)(2,1)} %shard_map.103), calls=%async_computation.2 | async-start | bytes 589824 | tf_op jit(solution)/shard_map/all_to_all | solution.py:317
  52.1 11.4 %copy-start.1 = (bf16[16,16,384]{2,1,0:T(8,128)(2,1)S(1)}, bf16[16,16,384]{2,1,0:T(8,128)(2,1)}, u32[]{:S(2)}) copy-start(bf16[16,16,384]{2,1,0:T(8,128)(2,1)} %fields_ref.1) | copy-start | bytes 589828
  59.5 46.0 %all-to-all-start.3 = ((bf16[32,60,128]{2,1,0:T(8,128)(2,1)}), bf16[32,60,128]{2,1,0:T(8,128)(2,1)S(1)}, u32[]{:S(2)}, u32[]{:S(2)}) async-start(bf16[32,60,128]{2,1,0:T(8,128)(2,1)} %shard_map.104), calls=%async_computation.3 | async-start | bytes 1048576 | tf_op jit(solution)/shard_map/all_to_all | solution.py:317
  63.4 26.2 %copy-start.13 = (f32[384]{0:T(512)S(1)}, f32[384]{0:T(512)}, u32[]{:S(2)}) copy-start(f32[384]{0:T(512)} %param.17) | copy-start | bytes 4612
  63.5 38.2 %copy-start.2 = (bf16[3,384,384]{2,1,0:T(8,128)(2,1)S(1)}, bf16[3,384,384]{2,1,0:T(8,128)(2,1)}, u32[]{:S(2)}) copy-start(bf16[3,384,384]{2,1,0:T(8,128)(2,1)} %mix_ref.2) | copy-start | bytes 2654212
  63.5 15.4 %collective-permute-start = (bf16[5,16,384]{2,1,0:T(8,128)(2,1)S(1)}, bf16[5,16,384]{2,1,0:T(8,128)(2,1)S(1)}, u32[]{:S(2)}, u32[]{:S(2)}) collective-permute-start(bf16[5,16,384]{2,1,0:T(8,128)(2,1)S(1)} %fusion.14), channel_id=1, source_target_pairs={{0,32},{32,64},{64,96},{96,128},{128,160},{160,192},{192,224},{224... | collective-permute-start | bytes 184328 | tf_op jit(solution)/shard_map/ppermute | solution.py:303
  66.3 12.6 %collective-permute-start.1 = (bf16[5,16,384]{2,1,0:T(8,128)(2,1)S(1)}, bf16[5,16,384]{2,1,0:T(8,128)(2,1)S(1)}, u32[]{:S(2)}, u32[]{:S(2)}) collective-permute-start(bf16[5,16,384]{2,1,0:T(8,128)(2,1)S(1)} %fusion.15), channel_id=1, source_target_pairs={{32,0},{64,32},{96,64},{128,96},{160,128},{192,160},{224,192},{256... | collective-permute-start | bytes 184328 | tf_op jit(solution)/shard_map/ppermute | solution.py:303
  79.0 14.9 %collective-permute-start.2 = (bf16[24,16,384]{2,1,0:T(8,128)(2,1)S(1)}, bf16[24,16,384]{2,1,0:T(8,128)(2,1)S(1)}, u32[]{:S(2)}, u32[]{:S(2)}) collective-permute-start(bf16[24,16,384]{2,1,0:T(8,128)(2,1)S(1)} %pad_maximum_fusion.rim_ref), channel_id=1, source_target_pairs={{0,1},{1,2},{2,3},{3,4},{4,5},{5,6},{6,7},{7,8},{8,9},{9,10},{10,1... | collective-permute-start | bytes 884744 | tf_op jit(solution)/shard_map/ppermute | solution.py:303
  82.0 18.9 %collective-permute-start.3 = (bf16[24,16,384]{2,1,0:T(8,128)(2,1)S(1)}, bf16[24,16,384]{2,1,0:T(8,128)(2,1)S(1)}, u32[]{:S(2)}, u32[]{:S(2)}) collective-permute-start(bf16[24,16,384]{2,1,0:T(8,128)(2,1)S(1)} %pad_maximum_fusion.rim_ref), channel_id=1, source_target_pairs={{0,31},{1,0},{2,1},{3,2},{4,3},{5,4},{6,5},{7,6},{8,7},{9,8},{10,9... | collective-permute-start | bytes 884744 | tf_op jit(solution)/shard_map/ppermute | solution.py:303
  89.8 15.7 %copy-start.4 = (bf16[384,768]{1,0:T(8,128)(2,1)S(1)}, bf16[384,768]{1,0:T(8,128)(2,1)}, u32[]{:S(2)}) copy-start(bf16[384,768]{1,0:T(8,128)(2,1)} %in_ref.1) | copy-start | bytes 1769476
  93.9 0.7 copy-start.6
  100.9 0.7 copy-start.8
  101.6 1.0 copy-start.7
  102.6 1.0 copy-start.9
  105.5 1.2 %copy-start.3 = (bf16[3,384,384]{2,1,0:T(8,128)(2,1)S(1)}, bf16[3,384,384]{2,1,0:T(8,128)(2,1)}, u32[]{:S(2)}) copy-start(bf16[3,384,384]{2,1,0:T(8,128)(2,1)} %mix_ref.3) | copy-start | bytes 2654212
  106.7 1.1 copy-start.5

commit v2 on v1

--- a/solution.py
+++ b/solution.py
@@ -27,15 +27,20 @@
 AX = A + 2 * RLAT
 JX = 32
 OFF = 8
+LANES = 256
+EDGE = 2 * RLAT
 F32 = jnp.float32
 BF = jnp.bfloat16
 NT = (((1,), (1,)), ((), ()))
-VMEM_LIMIT = 48 * 1024 * 1024
-
-
-def call(kernel, outs, scratch, *args, smem=(), flops=1_000_000, moved=1_000_000):
+VMEM_LIMIT = 14 * 1024 * 1024
+LAST_LIMIT = 61 * 1024 * 1024
+
+
+def call(kernel, outs, scratch, *args, smem=(), hbm=(), limit=VMEM_LIMIT, moved=1.0):
     specs = [
-        pl.BlockSpec(memory_space=pltpu.SMEM if i in smem else pltpu.VMEM)
+        pl.BlockSpec(
+            memory_space=pltpu.SMEM if i in smem else pltpu.HBM if i in hbm else pltpu.VMEM
+        )
         for i in range(len(args))
     ]
     out_specs = jax.tree.map(lambda _: pl.BlockSpec(memory_space=pltpu.VMEM), outs)
@@ -45,8 +50,10 @@
         in_specs=specs,
         out_specs=out_specs,
         scratch_shapes=scratch,
-        cost_estimate=pl.CostEstimate(flops=flops, bytes_accessed=moved, transcendentals=0),
-        compiler_params=pltpu.CompilerParams(vmem_limit_bytes=VMEM_LIMIT),
+        cost_estimate=pl.CostEstimate(
+            flops=0, bytes_accessed=int(moved * 3_400_000), transcendentals=0
+        ),
+        compiler_params=pltpu.CompilerParams(vmem_limit_bytes=limit),
     )(*args)
 
 
@@ -67,15 +74,63 @@
     return pieces
 
 
-def prep_kernel(fields_ref, out_ref, rows):
-    turned = fields_ref[...].reshape(A * N, C).astype(F32).T
-    for hi in range(2):
-        rows[pl.ds(hi, C, stride=2), :] = turned[:, hi * 128 : hi * 128 + 128]
+def prep_kernel(fields_ref, out_ref, field, rows, sems):
+    copies = [
+        pltpu.make_async_copy(
+            fields_ref.at[:, :, pl.ds(128 * g, 128)], field.at[g], sems.at[g]
+        )
+        for g in range(3)
+    ]
+    for copy in copies:
+        copy.start()
+    for g in range(3):
+        copies[g].wait()
+        turned = field[g].reshape(A * N, 128).astype(F32).T
+        for hi in range(2):
+            rows[pl.ds(256 * g + hi, 128, stride=2), :] = turned[:, hi * 128 : hi * 128 + 128]
     for d in range(PLON):
         out_ref[d] = rows[24 * d : 24 * d + 24, :].astype(BF)
 
 
-def table_kernel(order_ref, cos_ref, diag_ref, out_ref, rows):
+def twiddle_kernel(place_ref, u_ref, v_ref, c_ref, s_ref, iu_ref, iv_ref, ic_ref, is_ref):
+    lane = lax.broadcasted_iota(jnp.int32, (PLON, 2 * M), 1)
+    row = lax.broadcasted_iota(jnp.int32, (PLON, 2 * M), 0)
+    order = lane // 2
+
+    def turn(product):
+        return 2.0 * math.pi / NLON * (product & (NLON - 1)).astype(F32)
+
+    outer = turn(row * N * order + (lane & 1) * (NLON // 4))
+    cos, sin = jnp.cos(outer), -jnp.sin(outer)
+    scale = jnp.where(order == 0, 1.0, 2.0)
+    u_ref[...], v_ref[...] = cos, sin
+    iu_ref[...], iv_ref[...] = cos * scale, sin * scale
+    inner = turn((row - OFF) * order)
+    cos, sin = jnp.cos(inner), jnp.sin(inner)
+    ic_ref[...], is_ref[...] = cos, sin
+    c_ref[...], s_ref[...] = cos[OFF : OFF + N], sin[OFF : OFF + N]
+
+
+def place_taps(stencil_ref, reach_ref, out_ref, wide):
+    offset = lax.broadcasted_iota(jnp.int32, (A, TAPS), 1) - RLON
+    cycle = lax.broadcasted_iota(jnp.int32, (A, TAPS), 0)
+    reach = jnp.zeros((A, TAPS), jnp.int32)
+    for a in range(A):
+        reach = jnp.where(cycle == a, reach_ref[a], reach)
+    inside = jnp.abs(offset) <= reach
+    for k in range(KB):
+        total = None
+        for d in range(DLAT):
+            taps = jnp.where(inside, stencil_ref[k * DLAT + d].astype(F32), 0.0)
+            taps = jnp.concatenate([taps, jnp.zeros((A, LANES - TAPS), F32)], axis=1)
+            taps = pltpu.roll(taps, d * wide, 1) if d else taps
+            total = taps if total is None else total + taps
+        out_ref[k] = total
+
+
+def table_kernel(
+    order_ref, cos_ref, diag_ref, out_ref, rows
+):
     order = order_ref[...]
     square = order * order
     cosine = [jnp.broadcast_to(cos_ref[:, h * 128 : h * 128 + 128], (CP, 128)) for h in range(2)]
@@ -161,33 +216,29 @@
             at = (2 * m + r) * CL
             for h in range(2):
                 res[h, at : at + CL, :] = result[16 * r : 16 * r + CL, h * 128 : h * 128 + 128]
-    lanes = lax.broadcasted_iota(jnp.int32, (72, 128), 1)
-    place = lanes // 32
-    inner = lanes % 32
-    source = [[res.at[h][pl.ds(lo, 72, stride=4), :] for lo in range(4)] for h in range(2)]
+    lanes = lax.broadcasted_iota(jnp.int32, (48, 128), 1)
+    source = [[res.at[h][pl.ds(lo, 48, stride=6), :] for lo in range(6)] for h in range(2)]
     for j in range(PLAT):
         total = None
-        for lo in range(4):
-            shift = (lo * 32 - (16 * j - RLAT)) % 128
+        for lo in range(6):
+            shift = (lo * AX - (16 * j - RLAT)) % 128
             value = pltpu.roll(source[j // 8][lo], shift, 1) if shift else source[j // 8][lo]
             if j in (7, 8):
                 other = source[1 - j // 8][lo]
                 other = pltpu.roll(other, shift, 1) if shift else other
                 bound = 128 - (16 * 7 - RLAT) if j == 7 else RLAT
                 first, last = (value, other) if j == 7 else (other, value)
-                value = jnp.where(inner < bound, first, last)
-            total = value if total is None else jnp.where(place == lo, value, total)
+                value = jnp.where(lanes < lo * AX + bound, first, last)
+            total = value if total is None else jnp.where(lanes >= lo * AX, value, total)
         out_ref[j] = total.astype(BF)
 
 
 def inverse_kernel(recv_ref, u_ref, v_ref, c_ref, s_ref, out_ref, rows, coef, grid):
     for e in range(PLAT):
-        rows[72 * e : 72 * e + 72, :] = recv_ref[e].astype(F32)
-    for hi in range(3):
-        turned = rows[pl.ds(hi, 2 * M, stride=3), :].T
-        for lo in range(4):
-            at = (hi * 4 + lo) * AX
-            coef[at : at + AX, :] = turned[lo * 32 : lo * 32 + AX, :]
+        rows[48 * e : 48 * e + 48, :] = recv_ref[e].astype(F32)
+    for hi in range(2):
+        turned = rows[pl.ds(hi, 2 * M, stride=2), :].T
+        coef[hi * 6 * AX : (hi + 1) * 6 * AX, :] = turned[: 6 * AX, :]
     left = coef[...].astype(BF)
     cosb, sinb = c_ref[...], s_ref[...]
     for k in range(8):
@@ -207,13 +258,12 @@
 
 
 def gather_rows(taps_ref, field, mixing_ref, gathered, rows, cols, wide, start):
-    lanes = taps_ref.shape[1]
     for a in range(rows):
         bands = []
         for k in range(KB):
-            line = taps_ref[a * KB + k : a * KB + k + 1, :]
+            line = taps_ref[k, a : a + 1, :]
             band = pltpu.roll(
-                jnp.broadcast_to(line, (cols, lanes)), start, 1, stride=1, stride_axis=0
+                jnp.broadcast_to(line, (cols, LANES)), start, 1, stride=1, stride_axis=0
             )
             bands.append(band.astype(BF))
         band = jnp.concatenate(bands, axis=0)[:, : DLAT * wide]
@@ -228,22 +278,51 @@
     return total
 
 
-def first_kernel(rim_ref, left_ref, right_ref, taps_ref, mix_ref, out_ref, field, gathered):
-    for a in range(AX + 2 * RLAT):
-        field[48 * a : 48 * a + 16, :] = left_ref[a]
-        field[48 * a + 16 : 48 * a + 32, :] = rim_ref[a]
-        field[48 * a + 32 : 48 * a + 48, :] = right_ref[a]
-    first = gather_rows(taps_ref, field, mix_ref, gathered, AX, JX, 48, 16 - OFF - RLON)
+def edge_kernel(
+    fields_ref, left_ref, right_ref, stencil_ref, reach_ref, up_ref, down_ref, taps_ref
+):
+    place_taps(stencil_ref, reach_ref, taps_ref, 48)
+    for out_ref, first, line in ((up_ref, A - EDGE, A - RLAT), (down_ref, 0, 0)):
+        for a in range(EDGE):
+            for n, part in enumerate((left_ref, fields_ref, right_ref)):
+                out_ref[48 * a + 16 * n : 48 * a + 16 * n + 16, :] = part[first + a]
+        lines = [taps_ref[k, line : line + RLAT, :] for k in range(KB)]
+        lines = jnp.concatenate(lines + [jnp.zeros((16 - KB * RLAT, LANES), F32)], axis=0)
+        lines = jnp.concatenate([lines, jnp.zeros((16, C - LANES), F32)], axis=1)
+        out_ref[48 * EDGE : 48 * EDGE + 16, :] = lines.astype(BF)
+
+
+def first_kernel(
+    fields_ref, left_ref, right_ref, above_ref, below_ref, taps_ref, mix_ref, out_ref,
+    field, taps, gathered,
+):
+    field[: 48 * EDGE, :] = above_ref[: 48 * EDGE, :]
+    field[48 * (A + EDGE) :, :] = below_ref[: 48 * EDGE, :]
+    for a in range(A):
+        for n, part in enumerate((left_ref, fields_ref, right_ref)):
+            at = 48 * (a + EDGE) + 16 * n
+            field[at : at + 16, :] = part[a]
+    top = above_ref[48 * EDGE : 48 * EDGE + 16, :].astype(F32)
+    bottom = below_ref[48 * EDGE : 48 * EDGE + 16, :].astype(F32)
+    for k in range(KB):
+        part = slice(RLAT * k, RLAT * k + RLAT)
+        taps[k, :RLAT, :] = top[part, :LANES]
+        taps[k, RLAT : RLAT + A, :] = taps_ref[k]
+        taps[k, RLAT + A : AX, :] = bottom[part, :LANES]
+    first = gather_rows(taps, field, mix_ref, gathered, AX, JX, 48, 16 - OFF - RLON)
     for a in range(AX):
-        at = (a + RLAT) * 48 + 16 - OFF
         own = field[(a + RLAT) * 48 : (a + RLAT) * 48 + 48, :].astype(F32)
         out_ref[a * JX : (a + 1) * JX, :] = (
             first[a * JX : (a + 1) * JX] + own[16 - OFF : 16 - OFF + JX]
         )
 
 
+def lines_kernel(stencil_ref, reach_ref, taps_ref):
+    place_taps(stencil_ref, reach_ref, taps_ref, JX)
+
+
 def last_kernel(
-    place_ref, recv_ref, pre_ref, taps_ref, mix_ref, norm_ref, in_ref, back_ref, out_ref,
+    place_ref, recv_ref, pre_ref, taps_ref, norm_ref, mix_ref, in_ref, back_ref, out_ref,
     rows, stream, exact, gathered,
 ):
     place = place_ref[0]
@@ -269,22 +348,6 @@
     out_ref[...] = (own + update).astype(BF).reshape(A, N, C)
 
 
-def circle(product):
-    return 2.0 * math.pi / NLON * (product % NLON).astype(F32)
-
-
-def sector_tables(cells, doubled):
-    orders = jnp.arange(M, dtype=jnp.int32)
-    sectors = N * jnp.arange(PLON, dtype=jnp.int32)
-    outer = circle(sectors[:, None] * orders[None, :])
-    inner = circle(cells[:, None] * orders[None, :])
-    scale = jnp.where(orders == 0, 1.0, 2.0).astype(F32) if doubled else 1.0
-    cos, sin = jnp.cos(outer) * scale, jnp.sin(outer) * scale
-    u = jnp.stack([cos, -sin], axis=-1).reshape(PLON, 2 * M)
-    v = jnp.stack([-sin, -cos], axis=-1).reshape(PLON, 2 * M)
-    return u, v, jnp.repeat(jnp.cos(inner), 2, axis=1), jnp.repeat(jnp.sin(inner), 2, axis=1)
-
-
 def legendre_start(colatitude, orders, degrees):
     order_vals = orders.astype(F32)
     counter = jnp.arange(1, degrees + 1, dtype=jnp.int32).astype(F32)
@@ -301,16 +364,6 @@
     count = lax.axis_size(axis)
     pairs = [(i, (i + by) % count) for i in range(count) if closed or 0 <= i + by < count]
     return lax.ppermute(value, axis, pairs)
-
-
-def tap_lines(stencil, cycle_reach, wide, lanes):
-    rows = stencil.shape[0]
-    offsets = jnp.arange(TAPS, dtype=jnp.int32) - RLON
-    inside = (jnp.abs(offsets)[None, :] <= cycle_reach[:, None]).astype(BF)
-    masked = stencil * inside[:, None, None, :]
-    masked = jnp.pad(masked, ((0, 0), (0, 0), (0, 0), (0, wide - TAPS)))
-    masked = masked.reshape(rows, KB, DLAT * wide)
-    return jnp.pad(masked, ((0, 0), (0, 0), (0, lanes - DLAT * wide)))
 
 
 def exchange(block, axis):
@@ -332,84 +385,127 @@
     diagonal = legendre_start(colatitude, own_orders, M)
 
     sent = call(
-        prep_kernel, shape((PLON, 24, 128), BF), [pltpu.VMEM((768, 128), F32)], fields
-    )
+        prep_kernel,
+        shape((PLON, 24, 128), BF),
+        [
+            pltpu.VMEM((3, A, N, 128), BF),
+            pltpu.VMEM((768, 128), F32),
+            pltpu.SemaphoreType.DMA((3,)),
+        ],
+        fields,
+        hbm=(0,),
+        limit=LAST_LIMIT,
+        moved=1.1,
+    )
+    sent, late_place, own_fields = lax.optimization_barrier((sent, place.reshape(1), fields))
     recv = exchange(sent, "lon")
-
-    lines_one = tap_lines(stencil_one, cycle_reach, 48, 256)
-    lines_two = tap_lines(stencil_two, cycle_reach, JX, 256).reshape(A * KB, 256).astype(F32)
-    edge = 2 * RLAT
-
-    def packed(cells, lines):
-        extra = jnp.pad(lines.reshape(1, 4, C), ((0, 0), (0, N - 4), (0, 0)))
-        return jnp.concatenate([cells, extra], axis=0)
-
-    above = shifted(packed(fields[A - edge :], lines_one[A - RLAT :]), "lat", 1, False)
-    below = shifted(packed(fields[:edge], lines_one[:RLAT]), "lat", -1, False)
-    rim = jnp.concatenate([above[:edge], fields, below[:edge]], axis=0)
-    taps_one = (
-        jnp.concatenate(
-            [
-                above[edge, :4].reshape(RLAT, KB, 256),
-                lines_one,
-                below[edge, :4].reshape(RLAT, KB, 256),
-            ],
-            axis=0,
-        )
-        .reshape(AX * KB, 256)
-        .astype(F32)
-    )
-    left = shifted(rim, "lon", 1, True)
-    right = shifted(rim, "lon", -1, True)
-
-    table = call(
-        table_kernel,
-        shape((ML, M, NLAT), BF),
-        [pltpu.VMEM((2, M * CP, 128), F32)],
-        jnp.broadcast_to(own_orders.astype(F32)[:, None], (CP, 128)),
-        jnp.cos(colatitude)[None, :],
-        diagonal,
-    )
+    left = shifted(own_fields, "lon", 1, True)
+    right = shifted(own_fields, "lon", -1, True)
+    factors = call(
+        twiddle_kernel,
+        [
+            shape((rows, 2 * M), F32)
+            for rows in (PLON, PLON, N, N, PLON, PLON, JX, JX)
+        ],
+        [],
+        late_place,
+        smem=(0,),
+        moved=0.4,
+    )
+
+    def by_offset(stencil):
+        return jnp.transpose(stencil, (1, 2, 0, 3)).reshape(KB * DLAT, A, TAPS)
+
     spectra = call(
         forward_kernel,
         shape((PLAT, 48, 128), BF),
         [pltpu.VMEM((4, 256, 128), F32), pltpu.VMEM((768, 128), F32)],
         recv,
-        *sector_tables(jnp.arange(N, dtype=jnp.int32), False),
+        *factors[:4],
+        moved=1.4,
+    )
+    spectra, late_orders, left, right = lax.optimization_barrier(
+        (spectra, own_orders, left, right)
     )
     gathered = exchange(spectra, "lat")
+    table = call(
+        table_kernel,
+        shape((ML, M, NLAT), BF),
+        [pltpu.VMEM((2, M * CP, 128), F32)],
+        jnp.broadcast_to(late_orders.astype(F32)[:, None], (CP, 128)),
+        jnp.cos(colatitude)[None, :],
+        diagonal,
+        moved=3.3,
+    )
+    up, down, taps_one = call(
+        edge_kernel,
+        [shape((48 * EDGE + 16, C), BF)] * 2 + [shape((KB, A, LANES), F32)],
+        [],
+        own_fields,
+        left,
+        right,
+        by_offset(stencil_one),
+        cycle_reach,
+        smem=(4,),
+        moved=0.7,
+    )
+    gathered, up, down = lax.optimization_barrier((gathered, up, down))
     gain = jnp.pad(spectral_gain.T, ((0, CP - CL), (0, 0)))
     results = call(
         legendre_kernel,
-        shape((PLAT, 72, 128), BF),
+        shape((PLAT, 48, 128), BF),
         [pltpu.VMEM((2, 384, 128), F32), pltpu.VMEM((2, 288, 128), F32)],
         gathered,
         table,
         quad[None, :],
         jnp.concatenate([gain, gain], axis=0),
-    )
+        moved=2.6,
+    )
+    results, up, down = lax.optimization_barrier((results, up, down))
     returned = exchange(results, "lat")
+    above = shifted(up, "lat", 1, False)
+    below = shifted(down, "lat", -1, False)
+    returned, above, below = lax.optimization_barrier((returned, above, below))
     sectors = call(
         inverse_kernel,
         shape((PLON, 60, 128), BF),
         [
-            pltpu.VMEM((1152, 128), F32),
+            pltpu.VMEM((768, 128), F32),
             pltpu.VMEM((CL * AX, 2 * M), F32),
             pltpu.VMEM((8, CL * AX, 128), F32),
         ],
         returned,
-        *sector_tables(jnp.arange(JX, dtype=jnp.int32) - OFF, True),
+        *factors[4:],
+        moved=1.7,
     )
     spectral = exchange(sectors, "lon")
+
     pre = call(
         first_kernel,
         shape((AX * JX, C), F32),
-        [pltpu.VMEM(((AX + edge) * 48, C), BF), pltpu.VMEM((KB, AX * JX, C), BF)],
-        rim,
+        [
+            pltpu.VMEM(((AX + EDGE) * 48, C), BF),
+            pltpu.VMEM((KB, 24, LANES), F32),
+            pltpu.VMEM((KB, AX * JX, C), BF),
+        ],
+        own_fields,
         left,
         right,
+        above,
+        below,
         taps_one,
         mix_one,
+        moved=1.9,
+    )
+    pre, late_two = lax.optimization_barrier((pre, by_offset(stencil_two)))
+    taps_two = call(
+        lines_kernel,
+        shape((KB, A, LANES), F32),
+        [],
+        late_two,
+        cycle_reach,
+        smem=(1,),
+        moved=8.0,
     )
     return call(
         last_kernel,
@@ -423,12 +519,13 @@
         place.reshape(1),
         spectral,
         pre,
-        lines_two,
+        taps_two,
+        norm_gain[None, :],
         mix_two,
-        norm_gain[None, :],
         w_in,
         w_out,
         smem=(0,),
+        moved=2.7,
     )
 
 

time: 111 us -> 99.4 us (0.90)
  the two profiles are of different devices: /device:TPU:2 before, /device:TPU:18 now
where the time goes in v2:
time: 99.4 us; the launch traced here: 98.6 us
  starting transfers between devices  46.5 us (47%)
  waiting for transfers between devices  27.6 us (28%)
  Pallas kernels  17.8 us (18%)
  local copies, waits for them, and re-layouts  5.94 us (6%)
    all_to_all x4, starting transfers between devices, exchange(): return lax.all_to_all(block, axis, split_axis=0, concat_axis=0, tiled=True)  27.4 us
    all_to_all x4, waiting for transfers between devices, exchange(): return lax.all_to_all(block, axis, split_axis=0, concat_axis=0, tiled=True)  24.8 us
    ppermute x4, starting transfers between devices, shifted(): return lax.ppermute(value, axis, pairs)  19.1 us
    pallas_call x10, Pallas kernels, call(): pl.pallas_call(kernel, out_shape=outs, in_specs=specs, out_specs=out_spec...  17.8 us
    unnamed x36, local copies, waits for them, and re-layouts  5.85 us
    ppermute x4, waiting for transfers between devices, shifted(): return lax.ppermute(value, axis, pairs)  2.77 us
  transfers between devices with their start and end apart: 8, of which 5 were waited for; matrix products, arithmetic and copies ran while one was open for 1% of the time, Pallas kernels for 8%

profile of v2, /device:TPU:18, one launch (start us, length us, event | category | flops | bytes accessed | tf_op | source)
XLA Modules:
  0.0 98.6 jit_solution(9204454716405264675)
XLA Ops:
  0.0 1.9 %shard_map.100 = bf16[32,24,128]{2,1,0:T(8,128)(2,1)} custom-call(bf16[16,16,384]{2,1,0:T(8,128)(2,1)} %fields_ref.3), custom_call_target="tpu_custom_call" | custom-call | bytes 3740000 | tf_op jit(solution)/shard_map/pallas_call | solution.py:47
  1.9 4.3 %collective-permute-start = (bf16[16,16,384]{2,1,0:T(8,128)(2,1)}, bf16[16,16,384]{2,1,0:T(8,128)(2,1)S(1)}, u32[]{:S(2)}, u32[]{:S(2)}) collective-permute-start(bf16[16,16,384]{2,1,0:T(8,128)(2,1)} %fields_ref.3), channel_id=1, source_target_pairs={{0,1},{1,2},{2,3},{3,4},{4,5},{5,6},{6,7},{7,8},{8,9},{9,10},{10,1... | collective-permute-start | bytes 589832 | tf_op jit(solution)/shard_map/ppermute | solution.py:366
  6.2 8.4 %collective-permute-start.1 = (bf16[16,16,384]{2,1,0:T(8,128)(2,1)}, bf16[16,16,384]{2,1,0:T(8,128)(2,1)S(1)}, u32[]{:S(2)}, u32[]{:S(2)}) collective-permute-start(bf16[16,16,384]{2,1,0:T(8,128)(2,1)} %fields_ref.3), channel_id=1, source_target_pairs={{0,31},{1,0},{2,1},{3,2},{4,3},{5,4},{6,5},{7,6},{8,7},{9,8},{10,9... | collective-permute-start | bytes 589832 | tf_op jit(solution)/shard_map/ppermute | solution.py:366
  14.6 10.5 %all-to-all-start = ((bf16[32,24,128]{2,1,0:T(8,128)(2,1)}), bf16[32,24,128]{2,1,0:T(8,128)(2,1)S(1)}, u32[]{:S(2)}, u32[]{:S(2)}) async-start(bf16[32,24,128]{2,1,0:T(8,128)(2,1)} %shard_map.100), calls=%async_computation | async-start | bytes 393216 | tf_op jit(solution)/shard_map/all_to_all | solution.py:370
  25.2 0.4 shard_map.101
  25.6 0.2 select_reduce_fusion
  25.8 10.7 %all-to-all-done.recv_ref = bf16[32,24,128]{2,1,0:T(8,128)(2,1)S(1)} async-done(((bf16[32,24,128]{2,1,0:T(8,128)(2,1)}), bf16[32,24,128]{2,1,0:T(8,128)(2,1)S(1)}, u32[]{:S(2)}, u32[]{:S(2)}) %all-to-all-start) | async-done | bytes 196640 | tf_op jit(solution)/shard_map/all_to_all | solution.py:370
  36.5 1.4 %shard_map.102 = bf16[16,48,128]{2,1,0:T(8,128)(2,1)} custom-call(bf16[32,24,128]{2,1,0:T(8,128)(2,1)S(1)} %all-to-all-done.recv_ref, f32[32,384]{1,0:T(8,128)S(1)} %get-tuple-element.36.u_ref, f32[32,384]{1,0:T(8,128)S(1)} %get-tuple-element.37.v_ref, f32[16,384]{1,0:T(8,128)S(1)} %get-tuple-element.38.c_ref, f32[16,384]{1,0:T(8,128)S(1)} %get-tuple-element.39.s_ref), custom_call_target="tpu_custom_call" | custom-call | bytes 4760000 | tf_op jit(solution)/shard_map/pallas_call | solution.py:47
  37.9 4.9 %all-to-all-start.1 = ((bf16[16,48,128]{2,1,0:T(8,128)(2,1)}), bf16[16,48,128]{2,1,0:T(8,128)(2,1)S(1)}, u32[]{:S(2)}, u32[]{:S(2)}) async-start(bf16[16,48,128]{2,1,0:T(8,128)(2,1)} %shard_map.102), calls=%async_computation.1 | async-start | bytes 393216 | tf_op jit(solution)/shard_map/all_to_all | solution.py:370
  42.9 0.1 add_exponential_fusion.diag_ref
  43.0 0.1 broadcast_in_dim.16.order_ref
  43.0 3.2 %shard_map.104.tab_ref = bf16[12,192,256]{2,1,0:T(8,128)(2,1)S(1)} custom-call(f32[16,128]{1,0:T(8,128)S(1)} %broadcast_in_dim.16.order_ref, f32[1,256]{1,0:T(1,128)S(1)} %fusion.1.cos_ref, f32[16,256]{1,0:T(8,128)S(1)} %add_exponential_fusion.diag_ref), custom_call_target="tpu_custom_call" | custom-call | bytes 11220000 | tf_op jit(solution)/shard_map/pallas_call | solution.py:47
  46.3 0.7 shard_map.103
  47.0 0.8 all-to-all-done.1.recv_ref
  47.8 3.3 %shard_map.105 = bf16[16,48,128]{2,1,0:T(8,128)(2,1)} custom-call(bf16[16,48,128]{2,1,0:T(8,128)(2,1)S(1)} %all-to-all-done.1.recv_ref, bf16[12,192,256]{2,1,0:T(8,128)(2,1)S(1)} %shard_map.104.tab_ref, f32[1,256]{1,0:T(1,128)S(1)} %sine_multiply_fusion.quad_ref, f32[32,192]{1,0:T(8,128)S(1)} %pad_maximum_fusion.gain_ref), custom_call_target="tpu_custom_call" | custom-call | bytes 8840000 | tf_op jit(solution)/shard_map/pallas_call | solution.py:47
  51.1 5.9 %all-to-all-start.2 = ((bf16[16,48,128]{2,1,0:T(8,128)(2,1)}), bf16[16,48,128]{2,1,0:T(8,128)(2,1)S(1)}, u32[]{:S(2)}, u32[]{:S(2)}) async-start(bf16[16,48,128]{2,1,0:T(8,128)(2,1)} %shard_map.105), calls=%async_computation.2 | async-start | bytes 393216 | tf_op jit(solution)/shard_map/all_to_all | solution.py:370
  57.1 2.0 %collective-permute-start.2 = (bf16[208,384]{1,0:T(8,128)(2,1)S(1)}, bf16[208,384]{1,0:T(8,128)(2,1)S(1)}, u32[]{:S(2)}, u32[]{:S(2)}) collective-permute-start(bf16[208,384]{1,0:T(8,128)(2,1)S(1)} %get-tuple-element.51), channel_id=1, source_target_pairs={{0,32},{32,64},{64,96},{96,128},{128,160},{160,192},{192,224},{224... | collective-permute-start | bytes 479240 | tf_op jit(solution)/shard_map/ppermute | solution.py:366
  59.1 4.4 %collective-permute-start.3 = (bf16[208,384]{1,0:T(8,128)(2,1)S(1)}, bf16[208,384]{1,0:T(8,128)(2,1)S(1)}, u32[]{:S(2)}, u32[]{:S(2)}) collective-permute-start(bf16[208,384]{1,0:T(8,128)(2,1)S(1)} %get-tuple-element.52), channel_id=1, source_target_pairs={{32,0},{64,32},{96,64},{128,96},{160,128},{192,160},{224,192},{256... | collective-permute-start | bytes 479240 | tf_op jit(solution)/shard_map/ppermute | solution.py:366
  63.5 1.0 %collective-permute-done.2.above_ref = bf16[208,384]{1,0:T(8,128)(2,1)S(1)} collective-permute-done((bf16[208,384]{1,0:T(8,128)(2,1)S(1)}, bf16[208,384]{1,0:T(8,128)(2,1)S(1)}, u32[]{:S(2)}, u32[]{:S(2)}) %collective-permute-start.2) | collective-permute-done | bytes 159776 | tf_op jit(solution)/shard_map/ppermute | solution.py:366
  64.5 1.8 %collective-permute-done.3.below_ref = bf16[208,384]{1,0:T(8,128)(2,1)S(1)} collective-permute-done((bf16[208,384]{1,0:T(8,128)(2,1)S(1)}, bf16[208,384]{1,0:T(8,128)(2,1)S(1)}, u32[]{:S(2)}, u32[]{:S(2)}) %collective-permute-start.3) | collective-permute-done | bytes 159776 | tf_op jit(solution)/shard_map/ppermute | solution.py:366
  66.3 1.8 %shard_map.106 = bf16[32,60,128]{2,1,0:T(8,128)(2,1)} custom-call(bf16[16,48,128]{2,1,0:T(8,128)(2,1)S(1)} %all-to-all-done.2.recv_ref, f32[32,384]{1,0:T(8,128)S(1)} %get-tuple-element.54.u_ref, f32[32,384]{1,0:T(8,128)S(1)} %get-tuple-element.55.v_ref, f32[32,384]{1,0:T(8,128)S(1)} %get-tuple-element.56.c_ref, f32[32,384]{1,0:T(8,128)S(1)} %get-tuple-element.57.s_ref), custom_call_target="tpu_custom_call" | custom-call | bytes 5780000 | tf_op jit(solution)/shard_map/pallas_call | solution.py:47
  68.1 6.1 %all-to-all-start.3 = ((bf16[32,60,128]{2,1,0:T(8,128)(2,1)}), bf16[32,60,128]{2,1,0:T(8,128)(2,1)S(1)}, u32[]{:S(2)}, u32[]{:S(2)}) async-start(bf16[32,60,128]{2,1,0:T(8,128)(2,1)} %shard_map.106), calls=%async_computation.3 | async-start | bytes 1048576 | tf_op jit(solution)/shard_map/all_to_all | solution.py:370
  74.3 0.9 copy-done.4
  75.2 0.9 copy-done.6
  76.1 0.9 copy-done.10
  77.0 0.9 copy-done.12
  78.0 1.9 %shard_map.107.pre_ref = f32[640,384]{1,0:T(8,128)S(1)} custom-call(bf16[16,16,384]{2,1,0:T(8,128)(2,1)S(1)} %copy-done, bf16[16,16,384]{2,1,0:T(8,128)(2,1)S(1)} %copy-done.4, bf16[16,16,384]{2,1,0:T(8,128)(2,1)S(1)} %copy-done.6, bf16[208,384]{1,0:T(8,128)(2,1)S(1)} %copy-done.10, bf16[208,384]{1,0:T(8,128)(2,1)S(1)} %copy-done.12, ...), custom_call_target="tpu_custom_call" | custom-call | bytes 6460000 | tf_op jit(solution)/shard_map/pallas_call | solution.py:47
  79.9 0.6 shard_map.108.taps_ref
  80.5 13.4 %all-to-all-done.3.recv_ref = bf16[32,60,128]{2,1,0:T(8,128)(2,1)S(1)} async-done(((bf16[32,60,128]{2,1,0:T(8,128)(2,1)}), bf16[32,60,128]{2,1,0:T(8,128)(2,1)S(1)}, u32[]{:S(2)}, u32[]{:S(2)}) %all-to-all-start.3) | async-done | bytes 491552 | tf_op jit(solution)/shard_map/all_to_all | solution.py:370
  93.9 1.1 %copy-done.7 = bf16[384,768]{1,0:T(8,128)(2,1)S(1)} copy-done((bf16[384,768]{1,0:T(8,128)(2,1)S(1)}, bf16[384,768]{1,0:T(8,128)(2,1)}, u32[]{:S(2)}) %copy-start.7) | copy-done | bytes 589848
  94.9 1.1 %copy-done.8 = bf16[768,384]{1,0:T(8,128)(2,1)S(1)} copy-done((bf16[768,384]{1,0:T(8,128)(2,1)S(1)}, bf16[768,384]{1,0:T(8,128)(2,1)}, u32[]{:S(2)}) %copy-start.8) | copy-done | bytes 589848
  96.0 2.6 %shard_map.109 = bf16[16,16,384]{2,1,0:T(8,128)(2,1)} custom-call(s32[1]{0:T(128)} %bitcast.place_ref, bf16[32,60,128]{2,1,0:T(8,128)(2,1)S(1)} %all-to-all-done.3.recv_ref, f32[640,384]{1,0:T(8,128)S(1)} %shard_map.107.pre_ref, f32[3,16,256]{2,1,0:T(8,128)S(1)} %shard_map.108.taps_ref, f32[1,384]{1,0:T(1,128)S(1)} %broadcast_in_dim.19.norm_ref, ...), custom_call_target="tpu_custom_call" | custom-call | bytes 9180000 | tf_op jit(solution)/shard_map/pallas_call | solution.py:47
  (45 shorter events, 0.3 us)
Async XLA Ops:
  0.0 42.9 %copy-start.16 = (f32[192,12]{0,1:T(8,128)S(1)}, f32[192,12]{0,1:T(8,128)}, u32[]{:S(2)}) copy-start(f32[192,12]{0,1:T(8,128)} %param.11) | copy-start | bytes 27652
  1.9 36.0 %collective-permute-start = (bf16[16,16,384]{2,1,0:T(8,128)(2,1)}, bf16[16,16,384]{2,1,0:T(8,128)(2,1)S(1)}, u32[]{:S(2)}, u32[]{:S(2)}) collective-permute-start(bf16[16,16,384]{2,1,0:T(8,128)(2,1)} %fields_ref.3), channel_id=1, source_target_pairs={{0,1},{1,2},{2,3},{3,4},{4,5},{5,6},{6,7},{7,8},{8,9},{9,10},{10,1... | collective-permute-start | bytes 589832 | tf_op jit(solution)/shard_map/ppermute | solution.py:366
  6.2 31.7 %collective-permute-start.1 = (bf16[16,16,384]{2,1,0:T(8,128)(2,1)}, bf16[16,16,384]{2,1,0:T(8,128)(2,1)S(1)}, u32[]{:S(2)}, u32[]{:S(2)}) collective-permute-start(bf16[16,16,384]{2,1,0:T(8,128)(2,1)} %fields_ref.3), channel_id=1, source_target_pairs={{0,31},{1,0},{2,1},{3,2},{4,3},{5,4},{6,5},{7,6},{8,7},{9,8},{10,9... | collective-permute-start | bytes 589832 | tf_op jit(solution)/shard_map/ppermute | solution.py:366
  14.6 21.9 %all-to-all-start = ((bf16[32,24,128]{2,1,0:T(8,128)(2,1)}), bf16[32,24,128]{2,1,0:T(8,128)(2,1)S(1)}, u32[]{:S(2)}, u32[]{:S(2)}) async-start(bf16[32,24,128]{2,1,0:T(8,128)(2,1)} %shard_map.100), calls=%async_computation | async-start | bytes 393216 | tf_op jit(solution)/shard_map/all_to_all | solution.py:370
  25.0 21.3 %copy-start = (bf16[16,16,384]{2,1,0:T(8,128)(2,1)S(1)}, bf16[16,16,384]{2,1,0:T(8,128)(2,1)}, u32[]{:S(2)}) copy-start(bf16[16,16,384]{2,1,0:T(8,128)(2,1)} %fields_ref.3) | copy-start | bytes 589828
  25.0 21.3 %copy-start.14 = (bf16[16,3,5,13]{3,0,2,1:T(8,128)(2,1)S(1)}, bf16[16,3,5,13]{3,0,2,1:T(8,128)(2,1)}, u32[]{:S(2)}) copy-start(bf16[16,3,5,13]{3,0,2,1:T(8,128)(2,1)} %param.12) | copy-start | bytes 18724
  25.1 21.3 %copy-start.15 = (s32[16]{0:T(128)S(1)}, s32[16]{0:T(128)}, u32[]{:S(2)}) copy-start(s32[16]{0:T(128)} %reach_ref.3) | copy-start | bytes 196
  37.9 9.1 %copy-start.3 = (bf16[16,16,384]{2,1,0:T(8,128)(2,1)}, bf16[16,16,384]{2,1,0:T(8,128)(2,1)S(1)}, u32[]{:S(2)}) copy-start(bf16[16,16,384]{2,1,0:T(8,128)(2,1)S(1)} %collective-permute-done.left_ref) | copy-start | bytes 589828
  37.9 9.1 %copy-start.5 = (bf16[16,16,384]{2,1,0:T(8,128)(2,1)}, bf16[16,16,384]{2,1,0:T(8,128)(2,1)S(1)}, u32[]{:S(2)}) copy-start(bf16[16,16,384]{2,1,0:T(8,128)(2,1)S(1)} %collective-permute-done.1.right_ref) | copy-start | bytes 589828
  37.9 9.9 %all-to-all-start.1 = ((bf16[16,48,128]{2,1,0:T(8,128)(2,1)}), bf16[16,48,128]{2,1,0:T(8,128)(2,1)S(1)}, u32[]{:S(2)}, u32[]{:S(2)}) async-start(bf16[16,48,128]{2,1,0:T(8,128)(2,1)} %shard_map.102), calls=%async_computation.1 | async-start | bytes 393216 | tf_op jit(solution)/shard_map/all_to_all | solution.py:370
  51.1 23.1 %copy-start.17 = (f32[384]{0:T(512)S(1)}, f32[384]{0:T(512)}, u32[]{:S(2)}) copy-start(f32[384]{0:T(512)} %param.17) | copy-start | bytes 4612
  51.1 23.1 %copy-start.1 = (bf16[3,384,384]{2,1,0:T(8,128)(2,1)S(1)}, bf16[3,384,384]{2,1,0:T(8,128)(2,1)}, u32[]{:S(2)}) copy-start(bf16[3,384,384]{2,1,0:T(8,128)(2,1)} %mix_ref.2) | copy-start | bytes 2654212
  51.1 15.2 %all-to-all-start.2 = ((bf16[16,48,128]{2,1,0:T(8,128)(2,1)}), bf16[16,48,128]{2,1,0:T(8,128)(2,1)S(1)}, u32[]{:S(2)}, u32[]{:S(2)}) async-start(bf16[16,48,128]{2,1,0:T(8,128)(2,1)} %shard_map.105), calls=%async_computation.2 | async-start | bytes 393216 | tf_op jit(solution)/shard_map/all_to_all | solution.py:370
  57.1 7.5 %collective-permute-start.2 = (bf16[208,384]{1,0:T(8,128)(2,1)S(1)}, bf16[208,384]{1,0:T(8,128)(2,1)S(1)}, u32[]{:S(2)}, u32[]{:S(2)}) collective-permute-start(bf16[208,384]{1,0:T(8,128)(2,1)S(1)} %get-tuple-element.51), channel_id=1, source_target_pairs={{0,32},{32,64},{64,96},{96,128},{128,160},{160,192},{192,224},{224... | collective-permute-start | bytes 479240 | tf_op jit(solution)/shard_map/ppermute | solution.py:366
  59.1 7.2 %collective-permute-start.3 = (bf16[208,384]{1,0:T(8,128)(2,1)S(1)}, bf16[208,384]{1,0:T(8,128)(2,1)S(1)}, u32[]{:S(2)}, u32[]{:S(2)}) collective-permute-start(bf16[208,384]{1,0:T(8,128)(2,1)S(1)} %get-tuple-element.52), channel_id=1, source_target_pairs={{32,0},{64,32},{96,64},{128,96},{160,128},{192,160},{224,192},{256... | collective-permute-start | bytes 479240 | tf_op jit(solution)/shard_map/ppermute | solution.py:366
  64.5 9.7 %copy-start.9 = (bf16[208,384]{1,0:T(8,128)(2,1)}, bf16[208,384]{1,0:T(8,128)(2,1)S(1)}, u32[]{:S(2)}) copy-start(bf16[208,384]{1,0:T(8,128)(2,1)S(1)} %collective-permute-done.2.above_ref) | copy-start | bytes 479236
  66.3 7.9 %copy-start.11 = (bf16[208,384]{1,0:T(8,128)(2,1)}, bf16[208,384]{1,0:T(8,128)(2,1)S(1)}, u32[]{:S(2)}) copy-start(bf16[208,384]{1,0:T(8,128)(2,1)S(1)} %collective-permute-done.3.below_ref) | copy-start | bytes 479236
  68.1 25.8 %all-to-all-start.3 = ((bf16[32,60,128]{2,1,0:T(8,128)(2,1)}), bf16[32,60,128]{2,1,0:T(8,128)(2,1)S(1)}, u32[]{:S(2)}, u32[]{:S(2)}) async-start(bf16[32,60,128]{2,1,0:T(8,128)(2,1)} %shard_map.106), calls=%async_computation.3 | async-start | bytes 1048576 | tf_op jit(solution)/shard_map/all_to_all | solution.py:370
  74.3 0.9 copy-start.4
  75.2 0.9 copy-start.6
  76.1 0.9 copy-start.10
  77.0 0.9 copy-start.12
  77.9 1.9 %copy-start.13 = (bf16[16,3,5,13]{3,0,2,1:T(8,128)(2,1)S(1)}, bf16[16,3,5,13]{3,0,2,1:T(8,128)(2,1)}, u32[]{:S(2)}) copy-start(bf16[16,3,5,13]{3,0,2,1:T(8,128)(2,1)} %param.13) | copy-start | bytes 18724
  78.0 15.9 %copy-start.2 = (bf16[3,384,384]{2,1,0:T(8,128)(2,1)S(1)}, bf16[3,384,384]{2,1,0:T(8,128)(2,1)}, u32[]{:S(2)}) copy-start(bf16[3,384,384]{2,1,0:T(8,128)(2,1)} %mix_ref.3) | copy-start | bytes 2654212
  93.9 1.1 %copy-start.7 = (bf16[384,768]{1,0:T(8,128)(2,1)S(1)}, bf16[384,768]{1,0:T(8,128)(2,1)}, u32[]{:S(2)}) copy-start(bf16[384,768]{1,0:T(8,128)(2,1)} %in_ref.1) | copy-start | bytes 1769476
  94.9 1.1 %copy-start.8 = (bf16[768,384]{1,0:T(8,128)(2,1)S(1)}, bf16[768,384]{1,0:T(8,128)(2,1)}, u32[]{:S(2)}) copy-start(bf16[768,384]{1,0:T(8,128)(2,1)} %back_ref.1) | copy-start | bytes 1769476

commit v3 on v2

--- a/solution.py
+++ b/solution.py
@@ -29,6 +29,7 @@
 OFF = 8
 LANES = 256
 EDGE = 2 * RLAT
+HALO = 2 * RLON
 F32 = jnp.float32
 BF = jnp.bfloat16
 NT = (((1,), (1,)), ((), ()))
@@ -51,7 +52,7 @@
         out_specs=out_specs,
         scratch_shapes=scratch,
         cost_estimate=pl.CostEstimate(
-            flops=0, bytes_accessed=int(moved * 3_400_000), transcendentals=0
+            flops=int(moved * 500_000_000), bytes_accessed=int(moved * 3_400_000), transcendentals=0
         ),
         compiler_params=pltpu.CompilerParams(vmem_limit_bytes=limit),
     )(*args)
@@ -278,32 +279,48 @@
     return total
 
 
-def edge_kernel(
-    fields_ref, left_ref, right_ref, stencil_ref, reach_ref, up_ref, down_ref, taps_ref
-):
+def edge_kernel(fields_ref, stencil_ref, reach_ref, up_ref, down_ref, taps_ref):
     place_taps(stencil_ref, reach_ref, taps_ref, 48)
     for out_ref, first, line in ((up_ref, A - EDGE, A - RLAT), (down_ref, 0, 0)):
         for a in range(EDGE):
-            for n, part in enumerate((left_ref, fields_ref, right_ref)):
-                out_ref[48 * a + 16 * n : 48 * a + 16 * n + 16, :] = part[first + a]
+            out_ref[N * a : N * a + N, :] = fields_ref[first + a]
         lines = [taps_ref[k, line : line + RLAT, :] for k in range(KB)]
-        lines = jnp.concatenate(lines + [jnp.zeros((16 - KB * RLAT, LANES), F32)], axis=0)
-        lines = jnp.concatenate([lines, jnp.zeros((16, C - LANES), F32)], axis=1)
-        out_ref[48 * EDGE : 48 * EDGE + 16, :] = lines.astype(BF)
+        lines = jnp.concatenate(lines + [jnp.zeros((N - KB * RLAT, LANES), F32)], axis=0)
+        lines = jnp.concatenate([lines, jnp.zeros((N, C - LANES), F32)], axis=1)
+        out_ref[N * EDGE : N * EDGE + N, :] = lines.astype(BF)
+
+
+def rim_row(a, fields_ref, above_ref, below_ref):
+    if a < EDGE:
+        return above_ref[N * a : N * a + N, :]
+    if a < A + EDGE:
+        return fields_ref[a - EDGE]
+    return below_ref[N * (a - A - EDGE) : N * (a - A - EDGE) + N, :]
+
+
+def rim_kernel(fields_ref, above_ref, below_ref, left_ref, right_ref, ahead, behind):
+    for a in range(AX + EDGE):
+        row = rim_row(a, fields_ref, above_ref, below_ref).astype(F32)
+        ahead[HALO * a : HALO * a + HALO, :] = row[N - HALO :]
+        behind[HALO * a : HALO * a + HALO, :] = row[:HALO]
+    right_ref[...] = ahead[...].astype(BF)
+    left_ref[...] = behind[...].astype(BF)
 
 
 def first_kernel(
     fields_ref, left_ref, right_ref, above_ref, below_ref, taps_ref, mix_ref, out_ref,
-    field, taps, gathered,
+    field, taps, gathered, before, after,
 ):
-    field[: 48 * EDGE, :] = above_ref[: 48 * EDGE, :]
-    field[48 * (A + EDGE) :, :] = below_ref[: 48 * EDGE, :]
-    for a in range(A):
-        for n, part in enumerate((left_ref, fields_ref, right_ref)):
-            at = 48 * (a + EDGE) + 16 * n
-            field[at : at + 16, :] = part[a]
-    top = above_ref[48 * EDGE : 48 * EDGE + 16, :].astype(F32)
-    bottom = below_ref[48 * EDGE : 48 * EDGE + 16, :].astype(F32)
+    before[...] = left_ref[...].astype(F32)
+    after[...] = right_ref[...].astype(F32)
+    gap = jnp.zeros((N - HALO, C), F32)
+    for a in range(AX + EDGE):
+        part = slice(HALO * a, HALO * a + HALO)
+        own = rim_row(a, fields_ref, above_ref, below_ref).astype(F32)
+        row = jnp.concatenate([gap, before[part, :], own, after[part, :], gap], axis=0)
+        field[48 * a : 48 * a + 48, :] = row.astype(BF)
+    top = above_ref[N * EDGE : N * EDGE + N, :].astype(F32)
+    bottom = below_ref[N * EDGE : N * EDGE + N, :].astype(F32)
     for k in range(KB):
         part = slice(RLAT * k, RLAT * k + RLAT)
         taps[k, :RLAT, :] = top[part, :LANES]
@@ -312,9 +329,8 @@
     first = gather_rows(taps, field, mix_ref, gathered, AX, JX, 48, 16 - OFF - RLON)
     for a in range(AX):
         own = field[(a + RLAT) * 48 : (a + RLAT) * 48 + 48, :].astype(F32)
-        out_ref[a * JX : (a + 1) * JX, :] = (
-            first[a * JX : (a + 1) * JX] + own[16 - OFF : 16 - OFF + JX]
-        )
+        value = first[a * JX : (a + 1) * JX] + own[16 - OFF : 16 - OFF + JX]
+        out_ref[a * JX : (a + 1) * JX, :] = value.astype(BF)
 
 
 def lines_kernel(stencil_ref, reach_ref, taps_ref):
@@ -330,7 +346,7 @@
         rows[60 * s : 60 * s + 60, :] = recv_ref[s].astype(F32)
     for hi in range(5):
         spectral = rows[pl.ds(hi, C, stride=5), :].T
-        value = pre_ref[128 * hi : 128 * hi + 128, :] + spectral
+        value = pre_ref[128 * hi : 128 * hi + 128, :].astype(F32) + spectral
         row = lax.broadcasted_iota(jnp.int32, (128, C), 0) // JX + 4 * hi - RLAT + place * A
         value = jnp.where((row >= 0) & (row < NLAT), value, 0.0).astype(BF)
         stream[128 * hi : 128 * hi + 128, :] = value
@@ -397,10 +413,10 @@
         limit=LAST_LIMIT,
         moved=1.1,
     )
-    sent, late_place, own_fields = lax.optimization_barrier((sent, place.reshape(1), fields))
+    sent, late_place, late_orders = lax.optimization_barrier(
+        (sent, place.reshape(1), own_orders)
+    )
     recv = exchange(sent, "lon")
-    left = shifted(own_fields, "lon", 1, True)
-    right = shifted(own_fields, "lon", -1, True)
     factors = call(
         twiddle_kernel,
         [
@@ -416,18 +432,6 @@
     def by_offset(stencil):
         return jnp.transpose(stencil, (1, 2, 0, 3)).reshape(KB * DLAT, A, TAPS)
 
-    spectra = call(
-        forward_kernel,
-        shape((PLAT, 48, 128), BF),
-        [pltpu.VMEM((4, 256, 128), F32), pltpu.VMEM((768, 128), F32)],
-        recv,
-        *factors[:4],
-        moved=1.4,
-    )
-    spectra, late_orders, left, right = lax.optimization_barrier(
-        (spectra, own_orders, left, right)
-    )
-    gathered = exchange(spectra, "lat")
     table = call(
         table_kernel,
         shape((ML, M, NLAT), BF),
@@ -437,19 +441,29 @@
         diagonal,
         moved=3.3,
     )
+    recv, table = lax.optimization_barrier((recv, table))
+    spectra = call(
+        forward_kernel,
+        shape((PLAT, 48, 128), BF),
+        [pltpu.VMEM((4, 256, 128), F32), pltpu.VMEM((768, 128), F32)],
+        recv,
+        *factors[:4],
+        moved=1.4,
+    )
     up, down, taps_one = call(
         edge_kernel,
-        [shape((48 * EDGE + 16, C), BF)] * 2 + [shape((KB, A, LANES), F32)],
+        [shape((N * EDGE + N, C), BF)] * 2 + [shape((KB, A, LANES), F32)],
         [],
-        own_fields,
-        left,
-        right,
+        fields,
         by_offset(stencil_one),
         cycle_reach,
-        smem=(4,),
+        smem=(2,),
         moved=0.7,
     )
-    gathered, up, down = lax.optimization_barrier((gathered, up, down))
+    spectra, up, down = lax.optimization_barrier((spectra, up, down))
+    gathered = exchange(spectra, "lat")
+    above = shifted(up, "lat", 1, False)
+    below = shifted(down, "lat", -1, False)
     gain = jnp.pad(spectral_gain.T, ((0, CP - CL), (0, 0)))
     results = call(
         legendre_kernel,
@@ -461,11 +475,19 @@
         jnp.concatenate([gain, gain], axis=0),
         moved=2.6,
     )
-    results, up, down = lax.optimization_barrier((results, up, down))
+    results, above, below = lax.optimization_barrier((results, above, below))
     returned = exchange(results, "lat")
-    above = shifted(up, "lat", 1, False)
-    below = shifted(down, "lat", -1, False)
-    returned, above, below = lax.optimization_barrier((returned, above, below))
+    to_left, to_right = call(
+        rim_kernel,
+        [shape((HALO * (AX + EDGE), C), BF)] * 2,
+        [pltpu.VMEM((HALO * (AX + EDGE), C), F32)] * 2,
+        fields,
+        above,
+        below,
+        moved=0.5,
+    )
+    left = shifted(to_right, "lon", 1, True)
+    right = shifted(to_left, "lon", -1, True)
     sectors = call(
         inverse_kernel,
         shape((PLON, 60, 128), BF),
@@ -479,23 +501,24 @@
         moved=1.7,
     )
     spectral = exchange(sectors, "lon")
-
     pre = call(
         first_kernel,
-        shape((AX * JX, C), F32),
+        shape((AX * JX, C), BF),
         [
             pltpu.VMEM(((AX + EDGE) * 48, C), BF),
             pltpu.VMEM((KB, 24, LANES), F32),
             pltpu.VMEM((KB, AX * JX, C), BF),
+            pltpu.VMEM((HALO * (AX + EDGE), C), F32),
+            pltpu.VMEM((HALO * (AX + EDGE), C), F32),
         ],
-        own_fields,
+        fields,
         left,
         right,
         above,
         below,
         taps_one,
         mix_one,
-        moved=1.9,
+        moved=0.1,
     )
     pre, late_two = lax.optimization_barrier((pre, by_offset(stencil_two)))
     taps_two = call(
@@ -505,7 +528,7 @@
         late_two,
         cycle_reach,
         smem=(1,),
-        moved=8.0,
+        moved=20.0,
     )
     return call(
         last_kernel,

time: 99.4 us -> 92 us (0.926)
  the two profiles are of different devices: /device:TPU:18 before, /device:TPU:12 now
where the time goes in v3:
time: 92 us; the launch traced here: 91.3 us
  starting transfers between devices  46.5 us (51%)
  waiting for transfers between devices  25.9 us (28%)
  Pallas kernels  18.1 us (20%)
    all_to_all x4, starting transfers between devices, exchange(): return lax.all_to_all(block, axis, split_axis=0, concat_axis=0, tiled=True)  30.9 us
    all_to_all x4, waiting for transfers between devices, exchange(): return lax.all_to_all(block, axis, split_axis=0, concat_axis=0, tiled=True)  21.5 us
    pallas_call x11, Pallas kernels, call(): pl.pallas_call(kernel, out_shape=outs, in_specs=specs, out_specs=out_spec...  18.1 us
    ppermute x4, starting transfers between devices, shifted(): return lax.ppermute(value, axis, pairs)  15.6 us
    ppermute x4, waiting for transfers between devices, shifted(): return lax.ppermute(value, axis, pairs)  4.42 us
  transfers between devices with their start and end apart: 8, of which 4 were waited for; matrix products, arithmetic and copies ran while one was open for 1% of the time, Pallas kernels for 13%

profile of v3, /device:TPU:12, one launch (start us, length us, event | category | flops | bytes accessed | tf_op | source)
XLA Modules:
  0.0 91.3 jit_solution(16417109620923005387)
XLA Ops:
  0.0 0.0 copy-start.5
  0.0 0.0 copy-start.7
  0.0 1.9 %shard_map.100 = bf16[32,24,128]{2,1,0:T(8,128)(2,1)} custom-call(bf16[16,16,384]{2,1,0:T(8,128)(2,1)} %fields_ref.7), custom_call_target="tpu_custom_call" | custom-call | flops 550000000 | bytes 3740000 | tf_op jit(solution)/shard_map/pallas_call | solution.py:48
  2.0 15.1 %all-to-all-start = ((bf16[32,24,128]{2,1,0:T(8,128)(2,1)}), bf16[32,24,128]{2,1,0:T(8,128)(2,1)S(1)}, u32[]{:S(2)}, u32[]{:S(2)}) async-start(bf16[32,24,128]{2,1,0:T(8,128)(2,1)} %shard_map.100), calls=%async_computation | async-start | bytes 393216 | tf_op jit(solution)/shard_map/all_to_all | solution.py:386
  17.1 0.1 fusion.1.cos_ref
  17.2 0.2 select_reduce_fusion
  17.4 0.7 shard_map.104
  18.1 0.4 shard_map.102
  18.5 0.1 add_exponential_fusion.diag_ref
  18.6 0.1 broadcast_in_dim.16.order_ref
  18.6 3.2 %shard_map.101.tab_ref = bf16[12,192,256]{2,1,0:T(8,128)(2,1)S(1)} custom-call(f32[16,128]{1,0:T(8,128)S(1)} %broadcast_in_dim.16.order_ref, f32[1,256]{1,0:T(1,128)S(1)} %fusion.1.cos_ref, f32[16,256]{1,0:T(8,128)S(1)} %add_exponential_fusion.diag_ref), custom_call_target="tpu_custom_call" | custom-call | flops 1650000000 | bytes 11220000 | tf_op jit(solution)/shard_map/pallas_call | solution.py:48
  21.9 8.6 %all-to-all-done.recv_ref = bf16[32,24,128]{2,1,0:T(8,128)(2,1)S(1)} async-done(((bf16[32,24,128]{2,1,0:T(8,128)(2,1)}), bf16[32,24,128]{2,1,0:T(8,128)(2,1)S(1)}, u32[]{:S(2)}, u32[]{:S(2)}) %all-to-all-start) | async-done | bytes 196640 | tf_op jit(solution)/shard_map/all_to_all | solution.py:386
  30.5 1.4 %shard_map.103 = bf16[16,48,128]{2,1,0:T(8,128)(2,1)} custom-call(bf16[32,24,128]{2,1,0:T(8,128)(2,1)S(1)} %all-to-all-done.recv_ref, f32[32,384]{1,0:T(8,128)S(1)} %get-tuple-element.35.u_ref, f32[32,384]{1,0:T(8,128)S(1)} %get-tuple-element.36.v_ref, f32[16,384]{1,0:T(8,128)S(1)} %get-tuple-element.37.c_ref, f32[16,384]{1,0:T(8,128)S(1)} %get-tuple-element.38.s_ref), custom_call_target="tpu_custom_call" | custom-call | flops 700000000 | bytes 4760000 | tf_op jit(solution)/shard_map/pallas_call | solution.py:48
  31.9 5.7 %all-to-all-start.1 = ((bf16[16,48,128]{2,1,0:T(8,128)(2,1)}), bf16[16,48,128]{2,1,0:T(8,128)(2,1)S(1)}, u32[]{:S(2)}, u32[]{:S(2)}) async-start(bf16[16,48,128]{2,1,0:T(8,128)(2,1)} %shard_map.103), calls=%async_computation.1 | async-start | bytes 393216 | tf_op jit(solution)/shard_map/all_to_all | solution.py:386
  37.7 0.1 sine_multiply_fusion.quad_ref
  37.7 2.1 %collective-permute-start = (bf16[80,384]{1,0:T(8,128)(2,1)S(1)}, bf16[80,384]{1,0:T(8,128)(2,1)S(1)}, u32[]{:S(2)}, u32[]{:S(2)}) collective-permute-start(bf16[80,384]{1,0:T(8,128)(2,1)S(1)} %get-tuple-element.43), channel_id=1, source_target_pairs={{0,32},{32,64},{64,96},{96,128},{128,160},{160,192},{192,224},{224... | collective-permute-start | bytes 184328 | tf_op jit(solution)/shard_map/ppermute | solution.py:382
  39.8 3.5 %collective-permute-start.1 = (bf16[80,384]{1,0:T(8,128)(2,1)S(1)}, bf16[80,384]{1,0:T(8,128)(2,1)S(1)}, u32[]{:S(2)}, u32[]{:S(2)}) collective-permute-start(bf16[80,384]{1,0:T(8,128)(2,1)S(1)} %get-tuple-element.44), channel_id=1, source_target_pairs={{32,0},{64,32},{96,64},{128,96},{160,128},{192,160},{224,192},{256... | collective-permute-start | bytes 184328 | tf_op jit(solution)/shard_map/ppermute | solution.py:382
  43.3 3.3 %shard_map.105 = bf16[16,48,128]{2,1,0:T(8,128)(2,1)} custom-call(bf16[16,48,128]{2,1,0:T(8,128)(2,1)S(1)} %all-to-all-done.1.recv_ref, bf16[12,192,256]{2,1,0:T(8,128)(2,1)S(1)} %shard_map.101.tab_ref, f32[1,256]{1,0:T(1,128)S(1)} %sine_multiply_fusion.quad_ref, f32[32,192]{1,0:T(8,128)S(1)} %pad_maximum_fusion.gain_ref), custom_call_target="tpu_custom_call" | custom-call | flops 1300000000 | bytes 8840000 | tf_op jit(solution)/shard_map/pallas_call | solution.py:48
  46.7 6.0 %all-to-all-start.2 = ((bf16[16,48,128]{2,1,0:T(8,128)(2,1)}), bf16[16,48,128]{2,1,0:T(8,128)(2,1)S(1)}, u32[]{:S(2)}, u32[]{:S(2)}) async-start(bf16[16,48,128]{2,1,0:T(8,128)(2,1)} %shard_map.105), calls=%async_computation.2 | async-start | bytes 393216 | tf_op jit(solution)/shard_map/all_to_all | solution.py:386
  52.7 0.1 shard_map.107
  52.8 3.4 %collective-permute-start.2 = (bf16[288,384]{1,0:T(8,128)(2,1)S(1)}, bf16[288,384]{1,0:T(8,128)(2,1)S(1)}, u32[]{:S(2)}, u32[]{:S(2)}) collective-permute-start(bf16[288,384]{1,0:T(8,128)(2,1)S(1)} %get-tuple-element.52), channel_id=1, source_target_pairs={{0,1},{1,2},{2,3},{3,4},{4,5},{5,6},{6,7},{7,8},{8,9},{9,10},{10,1... | collective-permute-start | bytes 663560 | tf_op jit(solution)/shard_map/ppermute | solution.py:382
  56.2 6.7 %collective-permute-start.3 = (bf16[288,384]{1,0:T(8,128)(2,1)S(1)}, bf16[288,384]{1,0:T(8,128)(2,1)S(1)}, u32[]{:S(2)}, u32[]{:S(2)}) collective-permute-start(bf16[288,384]{1,0:T(8,128)(2,1)S(1)} %get-tuple-element.53), channel_id=1, source_target_pairs={{0,31},{1,0},{2,1},{3,2},{4,3},{5,4},{6,5},{7,6},{8,7},{9,8},{10,9... | collective-permute-start | bytes 663560 | tf_op jit(solution)/shard_map/ppermute | solution.py:382
  62.9 0.0 copy-start.9
  62.9 1.8 %shard_map.106 = bf16[32,60,128]{2,1,0:T(8,128)(2,1)} custom-call(bf16[16,48,128]{2,1,0:T(8,128)(2,1)S(1)} %all-to-all-done.2.recv_ref, f32[32,384]{1,0:T(8,128)S(1)} %get-tuple-element.46.u_ref, f32[32,384]{1,0:T(8,128)S(1)} %get-tuple-element.47.v_ref, f32[32,384]{1,0:T(8,128)S(1)} %get-tuple-element.48.c_ref, f32[32,384]{1,0:T(8,128)S(1)} %get-tuple-element.49.s_ref), custom_call_target="tpu_custom_call" | custom-call | flops 850000000 | bytes 5780000 | tf_op jit(solution)/shard_map/pallas_call | solution.py:48
  64.7 4.0 %all-to-all-start.3 = ((bf16[32,60,128]{2,1,0:T(8,128)(2,1)}), bf16[32,60,128]{2,1,0:T(8,128)(2,1)S(1)}, u32[]{:S(2)}, u32[]{:S(2)}) async-start(bf16[32,60,128]{2,1,0:T(8,128)(2,1)} %shard_map.106), calls=%async_computation.3 | async-start | bytes 1048576 | tf_op jit(solution)/shard_map/all_to_all | solution.py:386
  68.7 0.0 copy-start.6
  68.8 1.7 %collective-permute-done.2.left_ref = bf16[288,384]{1,0:T(8,128)(2,1)S(1)} collective-permute-done((bf16[288,384]{1,0:T(8,128)(2,1)S(1)}, bf16[288,384]{1,0:T(8,128)(2,1)S(1)}, u32[]{:S(2)}, u32[]{:S(2)}) %collective-permute-start.2) | collective-permute-done | bytes 221216 | tf_op jit(solution)/shard_map/ppermute | solution.py:382
  70.4 2.7 %collective-permute-done.3.right_ref = bf16[288,384]{1,0:T(8,128)(2,1)S(1)} collective-permute-done((bf16[288,384]{1,0:T(8,128)(2,1)S(1)}, bf16[288,384]{1,0:T(8,128)(2,1)S(1)}, u32[]{:S(2)}, u32[]{:S(2)}) %collective-permute-start.3) | collective-permute-done | bytes 221216 | tf_op jit(solution)/shard_map/ppermute | solution.py:382
  73.2 1.9 %shard_map.108.pre_ref = bf16[640,384]{1,0:T(8,128)(2,1)S(1)} custom-call(bf16[16,16,384]{2,1,0:T(8,128)(2,1)S(1)} %copy-done.1, bf16[288,384]{1,0:T(8,128)(2,1)S(1)} %collective-permute-done.2.left_ref, bf16[288,384]{1,0:T(8,128)(2,1)S(1)} %collective-permute-done.3.right_ref, bf16[80,384]{1,0:T(8,128)(2,1)S(1)} %collective-permute-done.above_ref, ...), custom_call_target="tpu_custom_call" | custom-call | flops 50000000 | bytes 340000 | tf_op jit(solution)/shard_map/pallas_call | solution.py:48
  75.1 0.6 shard_map.109.taps_ref
  75.8 12.8 %all-to-all-done.3.recv_ref = bf16[32,60,128]{2,1,0:T(8,128)(2,1)S(1)} async-done(((bf16[32,60,128]{2,1,0:T(8,128)(2,1)}), bf16[32,60,128]{2,1,0:T(8,128)(2,1)S(1)}, u32[]{:S(2)}, u32[]{:S(2)}) %all-to-all-start.3) | async-done | bytes 491552 | tf_op jit(solution)/shard_map/all_to_all | solution.py:386
  88.6 2.7 %shard_map.110 = bf16[16,16,384]{2,1,0:T(8,128)(2,1)} custom-call(s32[1]{0:T(128)} %bitcast.place_ref, bf16[32,60,128]{2,1,0:T(8,128)(2,1)S(1)} %all-to-all-done.3.recv_ref, bf16[640,384]{1,0:T(8,128)(2,1)S(1)} %shard_map.108.pre_ref, f32[3,16,256]{2,1,0:T(8,128)S(1)} %shard_map.109.taps_ref, f32[1,384]{1,0:T(1,128)S(1)} %broadcast_in_dim.19.norm_ref, ...), custom_call_target="tpu_custom_call" | custom-call | flops 1350000000 | bytes 9180000 | tf_op jit(solution)/shard_map/pallas_call | solution.py:48
  (29 shorter events, 0.2 us)
Async XLA Ops:
  0.0 17.4 %copy-start.1 = (bf16[16,16,384]{2,1,0:T(8,128)(2,1)S(1)}, bf16[16,16,384]{2,1,0:T(8,128)(2,1)}, u32[]{:S(2)}) copy-start(bf16[16,16,384]{2,1,0:T(8,128)(2,1)} %fields_ref.7) | copy-start | bytes 589828
  0.0 17.4 %copy-start.5 = (bf16[16,3,5,13]{3,0,2,1:T(8,128)(2,1)S(1)}, bf16[16,3,5,13]{3,0,2,1:T(8,128)(2,1)}, u32[]{:S(2)}) copy-start(bf16[16,3,5,13]{3,0,2,1:T(8,128)(2,1)} %param.12) | copy-start | bytes 18724
  0.0 17.4 %copy-start.7 = (s32[16]{0:T(128)S(1)}, s32[16]{0:T(128)}, u32[]{:S(2)}) copy-start(s32[16]{0:T(128)} %reach_ref.3) | copy-start | bytes 196
  2.0 28.6 %all-to-all-start = ((bf16[32,24,128]{2,1,0:T(8,128)(2,1)}), bf16[32,24,128]{2,1,0:T(8,128)(2,1)S(1)}, u32[]{:S(2)}, u32[]{:S(2)}) async-start(bf16[32,24,128]{2,1,0:T(8,128)(2,1)} %shard_map.100), calls=%async_computation | async-start | bytes 393216 | tf_op jit(solution)/shard_map/all_to_all | solution.py:386
  30.5 7.1 %copy-start.8 = (f32[192,12]{0,1:T(8,128)S(1)}, f32[192,12]{0,1:T(8,128)}, u32[]{:S(2)}) copy-start(f32[192,12]{0,1:T(8,128)} %param.11) | copy-start | bytes 27652
  31.9 11.4 %all-to-all-start.1 = ((bf16[16,48,128]{2,1,0:T(8,128)(2,1)}), bf16[16,48,128]{2,1,0:T(8,128)(2,1)S(1)}, u32[]{:S(2)}, u32[]{:S(2)}) async-start(bf16[16,48,128]{2,1,0:T(8,128)(2,1)} %shard_map.103), calls=%async_computation.1 | async-start | bytes 393216 | tf_op jit(solution)/shard_map/all_to_all | solution.py:386
  37.7 8.9 %collective-permute-start = (bf16[80,384]{1,0:T(8,128)(2,1)S(1)}, bf16[80,384]{1,0:T(8,128)(2,1)S(1)}, u32[]{:S(2)}, u32[]{:S(2)}) collective-permute-start(bf16[80,384]{1,0:T(8,128)(2,1)S(1)} %get-tuple-element.43), channel_id=1, source_target_pairs={{0,32},{32,64},{64,96},{96,128},{128,160},{160,192},{192,224},{224... | collective-permute-start | bytes 184328 | tf_op jit(solution)/shard_map/ppermute | solution.py:382
  39.8 6.9 %collective-permute-start.1 = (bf16[80,384]{1,0:T(8,128)(2,1)S(1)}, bf16[80,384]{1,0:T(8,128)(2,1)S(1)}, u32[]{:S(2)}, u32[]{:S(2)}) collective-permute-start(bf16[80,384]{1,0:T(8,128)(2,1)S(1)} %get-tuple-element.44), channel_id=1, source_target_pairs={{32,0},{64,32},{96,64},{128,96},{160,128},{192,160},{224,192},{256... | collective-permute-start | bytes 184328 | tf_op jit(solution)/shard_map/ppermute | solution.py:382
  46.7 16.2 %all-to-all-start.2 = ((bf16[16,48,128]{2,1,0:T(8,128)(2,1)}), bf16[16,48,128]{2,1,0:T(8,128)(2,1)S(1)}, u32[]{:S(2)}, u32[]{:S(2)}) async-start(bf16[16,48,128]{2,1,0:T(8,128)(2,1)} %shard_map.105), calls=%async_computation.2 | async-start | bytes 393216 | tf_op jit(solution)/shard_map/all_to_all | solution.py:386
  52.8 17.6 %collective-permute-start.2 = (bf16[288,384]{1,0:T(8,128)(2,1)S(1)}, bf16[288,384]{1,0:T(8,128)(2,1)S(1)}, u32[]{:S(2)}, u32[]{:S(2)}) collective-permute-start(bf16[288,384]{1,0:T(8,128)(2,1)S(1)} %get-tuple-element.52), channel_id=1, source_target_pairs={{0,1},{1,2},{2,3},{3,4},{4,5},{5,6},{6,7},{7,8},{8,9},{9,10},{10,1... | collective-permute-start | bytes 663560 | tf_op jit(solution)/shard_map/ppermute | solution.py:382
  56.2 16.9 %collective-permute-start.3 = (bf16[288,384]{1,0:T(8,128)(2,1)S(1)}, bf16[288,384]{1,0:T(8,128)(2,1)S(1)}, u32[]{:S(2)}, u32[]{:S(2)}) collective-permute-start(bf16[288,384]{1,0:T(8,128)(2,1)S(1)} %get-tuple-element.53), channel_id=1, source_target_pairs={{0,31},{1,0},{2,1},{3,2},{4,3},{5,4},{6,5},{7,6},{8,7},{9,8},{10,9... | collective-permute-start | bytes 663560 | tf_op jit(solution)/shard_map/ppermute | solution.py:382
  62.9 5.8 %copy-start.9 = (f32[384]{0:T(512)S(1)}, f32[384]{0:T(512)}, u32[]{:S(2)}) copy-start(f32[384]{0:T(512)} %param.17) | copy-start | bytes 4612
  64.7 8.5 %copy-start = (bf16[3,384,384]{2,1,0:T(8,128)(2,1)S(1)}, bf16[3,384,384]{2,1,0:T(8,128)(2,1)}, u32[]{:S(2)}) copy-start(bf16[3,384,384]{2,1,0:T(8,128)(2,1)} %mix_ref.2) | copy-start | bytes 2654212
  64.7 23.9 %all-to-all-start.3 = ((bf16[32,60,128]{2,1,0:T(8,128)(2,1)}), bf16[32,60,128]{2,1,0:T(8,128)(2,1)S(1)}, u32[]{:S(2)}, u32[]{:S(2)}) async-start(bf16[32,60,128]{2,1,0:T(8,128)(2,1)} %shard_map.106), calls=%async_computation.3 | async-start | bytes 1048576 | tf_op jit(solution)/shard_map/all_to_all | solution.py:386
  68.7 6.4 %copy-start.6 = (bf16[16,3,5,13]{3,0,2,1:T(8,128)(2,1)S(1)}, bf16[16,3,5,13]{3,0,2,1:T(8,128)(2,1)}, u32[]{:S(2)}) copy-start(bf16[16,3,5,13]{3,0,2,1:T(8,128)(2,1)} %param.13) | copy-start | bytes 18724
  75.1 13.5 %copy-start.2 = (bf16[3,384,384]{2,1,0:T(8,128)(2,1)S(1)}, bf16[3,384,384]{2,1,0:T(8,128)(2,1)}, u32[]{:S(2)}) copy-start(bf16[3,384,384]{2,1,0:T(8,128)(2,1)} %mix_ref.3) | copy-start | bytes 2654212
  75.1 13.5 %copy-start.3 = (bf16[384,768]{1,0:T(8,128)(2,1)S(1)}, bf16[384,768]{1,0:T(8,128)(2,1)}, u32[]{:S(2)}) copy-start(bf16[384,768]{1,0:T(8,128)(2,1)} %in_ref.1) | copy-start | bytes 1769476
  75.1 13.5 %copy-start.4 = (bf16[768,384]{1,0:T(8,128)(2,1)S(1)}, bf16[768,384]{1,0:T(8,128)(2,1)}, u32[]{:S(2)}) copy-start(bf16[768,384]{1,0:T(8,128)(2,1)} %back_ref.1) | copy-start | bytes 1769476

commit v4 on v3

--- a/solution.py
+++ b/solution.py
@@ -37,14 +37,14 @@
 LAST_LIMIT = 61 * 1024 * 1024
 
 
-def call(kernel, outs, scratch, *args, smem=(), hbm=(), limit=VMEM_LIMIT, moved=1.0):
+def call(kernel, outs, scratch, *args, smem=(), hbm=(), out=pltpu.VMEM, limit=VMEM_LIMIT, moved=1.0):
     specs = [
         pl.BlockSpec(
             memory_space=pltpu.SMEM if i in smem else pltpu.HBM if i in hbm else pltpu.VMEM
         )
         for i in range(len(args))
     ]
-    out_specs = jax.tree.map(lambda _: pl.BlockSpec(memory_space=pltpu.VMEM), outs)
+    out_specs = jax.tree.map(lambda _: pl.BlockSpec(memory_space=out), outs)
     return pl.pallas_call(
         kernel,
         out_shape=outs,
@@ -75,7 +75,14 @@
     return pieces
 
 
-def prep_kernel(fields_ref, out_ref, field, rows, sems):
+def send(stage, out_ref, sems, number, first, count):
+    part = pl.ds(first, count)
+    copy = pltpu.make_async_copy(stage.at[part], out_ref.at[part], sems.at[number])
+    copy.start()
+    return copy
+
+
+def prep_kernel(fields_ref, out_ref, field, rows, sems, stage, out_sems):
     copies = [
         pltpu.make_async_copy(
             fields_ref.at[:, :, pl.ds(128 * g, 128)], field.at[g], sems.at[g]
@@ -89,8 +96,12 @@
         turned = field[g].reshape(A * N, 128).astype(F32).T
         for hi in range(2):
             rows[pl.ds(256 * g + hi, 128, stride=2), :] = turned[:, hi * 128 : hi * 128 + 128]
-    for d in range(PLON):
-        out_ref[d] = rows[24 * d : 24 * d + 24, :].astype(BF)
+        first, last = ((0, 10), (10, 21), (21, PLON))[g]
+        for d in range(first, last):
+            stage[d] = rows[24 * d : 24 * d + 24, :].astype(BF)
+        copies.append(send(stage, out_ref, out_sems, g, first, last - first))
+    for copy in copies[3:]:
+        copy.wait()
 
 
 def twiddle_kernel(place_ref, u_ref, v_ref, c_ref, s_ref, iu_ref, iv_ref, ic_ref, is_ref):
@@ -162,7 +173,9 @@
             ].astype(BF)
 
 
-def forward_kernel(recv_ref, u_ref, v_ref, c_ref, s_ref, out_ref, grid, rows):
+def forward_kernel(
+    recv_ref, u_ref, v_ref, c_ref, s_ref, out_ref, grid, rows, stage, out_sems
+):
     pieces = [
         jnp.concatenate([recv_ref[hi * 8 + lo].astype(F32) for hi in range(4)], axis=0)
         for lo in range(8)
@@ -181,11 +194,18 @@
         ],
         axis=0,
     )
-    spectra = jnp.dot(circles, table, preferred_element_type=F32).T
-    for g in range(2):
-        rows[pl.ds(g, 2 * M, stride=2), :] = spectra[:, g * 128 : g * 128 + 128]
-    for e in range(PLAT):
-        out_ref[e] = rows[48 * e : 48 * e + 48, :].astype(BF)
+    spectra = jnp.dot(circles, table, preferred_element_type=F32)
+    copies = []
+    for b in range(3):
+        turned = spectra[:, 128 * b : 128 * b + 128].T
+        for g in range(2):
+            rows[pl.ds(256 * b + g, 128, stride=2), :] = turned[:, g * 128 : g * 128 + 128]
+        first, last = ((0, 5), (5, 10), (10, PLAT))[b]
+        for e in range(first, last):
+            stage[e] = rows[48 * e : 48 * e + 48, :].astype(BF)
+        copies.append(send(stage, out_ref, out_sems, b, first, last - first))
+    for copy in copies:
+        copy.wait()
 
 
 def split(value):
@@ -194,7 +214,9 @@
     return jnp.concatenate([high, low], axis=0)
 
 
-def legendre_kernel(recv_ref, tab_ref, quad_ref, gain_ref, out_ref, grid, res):
+def legendre_kernel(
+    recv_ref, tab_ref, quad_ref, gain_ref, out_ref, grid, res, stage, out_sems
+):
     pieces = [
         jnp.concatenate([recv_ref[hi * 8 + lo].astype(F32) for hi in range(2)], axis=0)
         for lo in range(8)
@@ -219,6 +241,7 @@
                 res[h, at : at + CL, :] = result[16 * r : 16 * r + CL, h * 128 : h * 128 + 128]
     lanes = lax.broadcasted_iota(jnp.int32, (48, 128), 1)
     source = [[res.at[h][pl.ds(lo, 48, stride=6), :] for lo in range(6)] for h in range(2)]
+    copies = []
     for j in range(PLAT):
         total = None
         for lo in range(6):
@@ -231,10 +254,16 @@
                 first, last = (value, other) if j == 7 else (other, value)
                 value = jnp.where(lanes < lo * AX + bound, first, last)
             total = value if total is None else jnp.where(lanes >= lo * AX, value, total)
-        out_ref[j] = total.astype(BF)
-
-
-def inverse_kernel(recv_ref, u_ref, v_ref, c_ref, s_ref, out_ref, rows, coef, grid):
+        stage[j] = total.astype(BF)
+        if j % 4 == 3:
+            copies.append(send(stage, out_ref, out_sems, j // 4, j - 3, 4))
+    for copy in copies:
+        copy.wait()
+
+
+def inverse_kernel(
+    recv_ref, u_ref, v_ref, c_ref, s_ref, out_ref, rows, coef, grid, stage, out_sems
+):
     for e in range(PLAT):
         rows[48 * e : 48 * e + 48, :] = recv_ref[e].astype(F32)
     for hi in range(2):
@@ -242,6 +271,7 @@
         coef[hi * 6 * AX : (hi + 1) * 6 * AX, :] = turned[: 6 * AX, :]
     left = coef[...].astype(BF)
     cosb, sinb = c_ref[...], s_ref[...]
+    copies = []
     for k in range(8):
         table = jnp.concatenate(
             [
@@ -251,11 +281,13 @@
             axis=0,
         )
         grid[k] = lax.dot_general(left, table, NT, preferred_element_type=F32)
-    for k in range(8):
         pieces = [grid.at[k][pl.ds(lo, 60, stride=4), :] for lo in range(4)]
         pieces = swap_blocks(pieces, 32)
         for lo in range(4):
-            out_ref[4 * k + lo] = pieces[lo].astype(BF)
+            stage[4 * k + lo] = pieces[lo].astype(BF)
+        copies.append(send(stage, out_ref, out_sems, k, 4 * k, 4))
+    for copy in copies:
+        copy.wait()
 
 
 def gather_rows(taps_ref, field, mixing_ref, gathered, rows, cols, wide, start):
@@ -407,8 +439,11 @@
             pltpu.VMEM((3, A, N, 128), BF),
             pltpu.VMEM((768, 128), F32),
             pltpu.SemaphoreType.DMA((3,)),
+            pltpu.VMEM((PLON, 24, 128), BF),
+            pltpu.SemaphoreType.DMA((3,)),
         ],
         fields,
+        out=pl.ANY,
         hbm=(0,),
         limit=LAST_LIMIT,
         moved=1.1,
@@ -445,9 +480,15 @@
     spectra = call(
         forward_kernel,
         shape((PLAT, 48, 128), BF),
-        [pltpu.VMEM((4, 256, 128), F32), pltpu.VMEM((768, 128), F32)],
+        [
+            pltpu.VMEM((4, 256, 128), F32),
+            pltpu.VMEM((768, 128), F32),
+            pltpu.VMEM((PLAT, 48, 128), BF),
+            pltpu.SemaphoreType.DMA((3,)),
+        ],
         recv,
         *factors[:4],
+        out=pl.ANY,
         moved=1.4,
     )
     up, down, taps_one = call(
@@ -468,11 +509,17 @@
     results = call(
         legendre_kernel,
         shape((PLAT, 48, 128), BF),
-        [pltpu.VMEM((2, 384, 128), F32), pltpu.VMEM((2, 288, 128), F32)],
+        [
+            pltpu.VMEM((2, 384, 128), F32),
+            pltpu.VMEM((2, 288, 128), F32),
+            pltpu.VMEM((PLAT, 48, 128), BF),
+            pltpu.SemaphoreType.DMA((4,)),
+        ],
         gathered,
         table,
         quad[None, :],
         jnp.concatenate([gain, gain], axis=0),
+        out=pl.ANY,
         moved=2.6,
     )
     results, above, below = lax.optimization_barrier((results, above, below))
@@ -495,9 +542,12 @@
             pltpu.VMEM((768, 128), F32),
             pltpu.VMEM((CL * AX, 2 * M), F32),
             pltpu.VMEM((8, CL * AX, 128), F32),
+            pltpu.VMEM((PLON, 60, 128), BF),
+            pltpu.SemaphoreType.DMA((8,)),
         ],
         returned,
         *factors[4:],
+        out=pl.ANY,
         moved=1.7,
     )
     spectral = exchange(sectors, "lon")

time: 92 us -> 92 us (level)
  no operation moved by 1% of the time
where the time goes in v4:
time: 92 us; the launch traced here: 91.3 us
  starting transfers between devices  46.5 us (51%)
  waiting for transfers between devices  25.9 us (28%)
  Pallas kernels  18 us (20%)
    all_to_all x4, starting transfers between devices, exchange(): return lax.all_to_all(block, axis, split_axis=0, concat_axis=0, tiled=True)  30.9 us
    all_to_all x4, waiting for transfers between devices, exchange(): return lax.all_to_all(block, axis, split_axis=0, concat_axis=0, tiled=True)  21.6 us
    pallas_call x11, Pallas kernels, call(): pl.pallas_call(kernel, out_shape=outs, in_specs=specs, out_specs=out_spec...  18 us
    ppermute x4, starting transfers between devices, shifted(): return lax.ppermute(value, axis, pairs)  15.6 us
    ppermute x4, waiting for transfers between devices, shifted(): return lax.ppermute(value, axis, pairs)  4.36 us
  transfers between devices with their start and end apart: 8, of which 4 were waited for; matrix products, arithmetic and copies ran while one was open for 1% of the time, Pallas kernels for 13%

profile of v4, /device:TPU:12, one launch (start us, length us, event | category | flops | bytes accessed | tf_op | source)
XLA Modules:
  0.0 91.3 jit_solution(14723501912569759623)
XLA Ops:
  0.0 0.0 copy-start.5
  0.0 0.0 copy-start.7
  0.0 1.9 %shard_map.100 = bf16[32,24,128]{2,1,0:T(8,128)(2,1)} custom-call(bf16[16,16,384]{2,1,0:T(8,128)(2,1)} %fields_ref.7), custom_call_target="tpu_custom_call" | custom-call | flops 550000000 | bytes 3740000 | tf_op jit(solution)/shard_map/pallas_call | solution.py:48
  2.0 15.1 %all-to-all-start = ((bf16[32,24,128]{2,1,0:T(8,128)(2,1)}), bf16[32,24,128]{2,1,0:T(8,128)(2,1)S(1)}, u32[]{:S(2)}, u32[]{:S(2)}) async-start(bf16[32,24,128]{2,1,0:T(8,128)(2,1)} %shard_map.100), calls=%async_computation | async-start | bytes 393216 | tf_op jit(solution)/shard_map/all_to_all | solution.py:418
  17.1 0.1 fusion.1.cos_ref
  17.2 0.2 select_reduce_fusion
  17.4 0.7 shard_map.104
  18.1 0.4 shard_map.102
  18.5 0.1 add_exponential_fusion.diag_ref
  18.6 0.1 broadcast_in_dim.16.order_ref
  18.6 3.2 %shard_map.101.tab_ref = bf16[12,192,256]{2,1,0:T(8,128)(2,1)S(1)} custom-call(f32[16,128]{1,0:T(8,128)S(1)} %broadcast_in_dim.16.order_ref, f32[1,256]{1,0:T(1,128)S(1)} %fusion.1.cos_ref, f32[16,256]{1,0:T(8,128)S(1)} %add_exponential_fusion.diag_ref), custom_call_target="tpu_custom_call" | custom-call | flops 1650000000 | bytes 11220000 | tf_op jit(solution)/shard_map/pallas_call | solution.py:48
  21.9 8.6 %all-to-all-done.recv_ref = bf16[32,24,128]{2,1,0:T(8,128)(2,1)S(1)} async-done(((bf16[32,24,128]{2,1,0:T(8,128)(2,1)}), bf16[32,24,128]{2,1,0:T(8,128)(2,1)S(1)}, u32[]{:S(2)}, u32[]{:S(2)}) %all-to-all-start) | async-done | bytes 196640 | tf_op jit(solution)/shard_map/all_to_all | solution.py:418
  30.5 1.4 %shard_map.103 = bf16[16,48,128]{2,1,0:T(8,128)(2,1)} custom-call(bf16[32,24,128]{2,1,0:T(8,128)(2,1)S(1)} %all-to-all-done.recv_ref, f32[32,384]{1,0:T(8,128)S(1)} %get-tuple-element.35.u_ref, f32[32,384]{1,0:T(8,128)S(1)} %get-tuple-element.36.v_ref, f32[16,384]{1,0:T(8,128)S(1)} %get-tuple-element.37.c_ref, f32[16,384]{1,0:T(8,128)S(1)} %get-tuple-element.38.s_ref), custom_call_target="tpu_custom_call" | custom-call | flops 700000000 | bytes 4760000 | tf_op jit(solution)/shard_map/pallas_call | solution.py:48
  32.0 5.7 %all-to-all-start.1 = ((bf16[16,48,128]{2,1,0:T(8,128)(2,1)}), bf16[16,48,128]{2,1,0:T(8,128)(2,1)S(1)}, u32[]{:S(2)}, u32[]{:S(2)}) async-start(bf16[16,48,128]{2,1,0:T(8,128)(2,1)} %shard_map.103), calls=%async_computation.1 | async-start | bytes 393216 | tf_op jit(solution)/shard_map/all_to_all | solution.py:418
  37.7 0.1 sine_multiply_fusion.quad_ref
  37.8 2.1 %collective-permute-start = (bf16[80,384]{1,0:T(8,128)(2,1)S(1)}, bf16[80,384]{1,0:T(8,128)(2,1)S(1)}, u32[]{:S(2)}, u32[]{:S(2)}) collective-permute-start(bf16[80,384]{1,0:T(8,128)(2,1)S(1)} %get-tuple-element.43), channel_id=1, source_target_pairs={{0,32},{32,64},{64,96},{96,128},{128,160},{160,192},{192,224},{224... | collective-permute-start | bytes 184328 | tf_op jit(solution)/shard_map/ppermute | solution.py:414
  39.9 3.5 %collective-permute-start.1 = (bf16[80,384]{1,0:T(8,128)(2,1)S(1)}, bf16[80,384]{1,0:T(8,128)(2,1)S(1)}, u32[]{:S(2)}, u32[]{:S(2)}) collective-permute-start(bf16[80,384]{1,0:T(8,128)(2,1)S(1)} %get-tuple-element.44), channel_id=1, source_target_pairs={{32,0},{64,32},{96,64},{128,96},{160,128},{192,160},{224,192},{256... | collective-permute-start | bytes 184328 | tf_op jit(solution)/shard_map/ppermute | solution.py:414
  43.4 3.3 %shard_map.105 = bf16[16,48,128]{2,1,0:T(8,128)(2,1)} custom-call(bf16[16,48,128]{2,1,0:T(8,128)(2,1)S(1)} %all-to-all-done.1.recv_ref, bf16[12,192,256]{2,1,0:T(8,128)(2,1)S(1)} %shard_map.101.tab_ref, f32[1,256]{1,0:T(1,128)S(1)} %sine_multiply_fusion.quad_ref, f32[32,192]{1,0:T(8,128)S(1)} %pad_maximum_fusion.gain_ref), custom_call_target="tpu_custom_call" | custom-call | flops 1300000000 | bytes 8840000 | tf_op jit(solution)/shard_map/pallas_call | solution.py:48
  46.7 6.0 %all-to-all-start.2 = ((bf16[16,48,128]{2,1,0:T(8,128)(2,1)}), bf16[16,48,128]{2,1,0:T(8,128)(2,1)S(1)}, u32[]{:S(2)}, u32[]{:S(2)}) async-start(bf16[16,48,128]{2,1,0:T(8,128)(2,1)} %shard_map.105), calls=%async_computation.2 | async-start | bytes 393216 | tf_op jit(solution)/shard_map/all_to_all | solution.py:418
  52.8 0.1 shard_map.107
  52.9 3.4 %collective-permute-start.2 = (bf16[288,384]{1,0:T(8,128)(2,1)S(1)}, bf16[288,384]{1,0:T(8,128)(2,1)S(1)}, u32[]{:S(2)}, u32[]{:S(2)}) collective-permute-start(bf16[288,384]{1,0:T(8,128)(2,1)S(1)} %get-tuple-element.52), channel_id=1, source_target_pairs={{0,1},{1,2},{2,3},{3,4},{4,5},{5,6},{6,7},{7,8},{8,9},{9,10},{10,1... | collective-permute-start | bytes 663560 | tf_op jit(solution)/shard_map/ppermute | solution.py:414
  56.3 6.7 %collective-permute-start.3 = (bf16[288,384]{1,0:T(8,128)(2,1)S(1)}, bf16[288,384]{1,0:T(8,128)(2,1)S(1)}, u32[]{:S(2)}, u32[]{:S(2)}) collective-permute-start(bf16[288,384]{1,0:T(8,128)(2,1)S(1)} %get-tuple-element.53), channel_id=1, source_target_pairs={{0,31},{1,0},{2,1},{3,2},{4,3},{5,4},{6,5},{7,6},{8,7},{9,8},{10,9... | collective-permute-start | bytes 663560 | tf_op jit(solution)/shard_map/ppermute | solution.py:414
  63.0 1.7 %shard_map.106 = bf16[32,60,128]{2,1,0:T(8,128)(2,1)} custom-call(bf16[16,48,128]{2,1,0:T(8,128)(2,1)S(1)} %all-to-all-done.2.recv_ref, f32[32,384]{1,0:T(8,128)S(1)} %get-tuple-element.46.u_ref, f32[32,384]{1,0:T(8,128)S(1)} %get-tuple-element.47.v_ref, f32[32,384]{1,0:T(8,128)S(1)} %get-tuple-element.48.c_ref, f32[32,384]{1,0:T(8,128)S(1)} %get-tuple-element.49.s_ref), custom_call_target="tpu_custom_call" | custom-call | flops 850000000 | bytes 5780000 | tf_op jit(solution)/shard_map/pallas_call | solution.py:48
  64.7 0.0 copy-start
  64.7 4.0 %all-to-all-start.3 = ((bf16[32,60,128]{2,1,0:T(8,128)(2,1)}), bf16[32,60,128]{2,1,0:T(8,128)(2,1)S(1)}, u32[]{:S(2)}, u32[]{:S(2)}) async-start(bf16[32,60,128]{2,1,0:T(8,128)(2,1)} %shard_map.106), calls=%async_computation.3 | async-start | bytes 1048576 | tf_op jit(solution)/shard_map/all_to_all | solution.py:418
  68.8 1.8 %collective-permute-done.2.left_ref = bf16[288,384]{1,0:T(8,128)(2,1)S(1)} collective-permute-done((bf16[288,384]{1,0:T(8,128)(2,1)S(1)}, bf16[288,384]{1,0:T(8,128)(2,1)S(1)}, u32[]{:S(2)}, u32[]{:S(2)}) %collective-permute-start.2) | collective-permute-done | bytes 221216 | tf_op jit(solution)/shard_map/ppermute | solution.py:414
  70.5 2.6 %collective-permute-done.3.right_ref = bf16[288,384]{1,0:T(8,128)(2,1)S(1)} collective-permute-done((bf16[288,384]{1,0:T(8,128)(2,1)S(1)}, bf16[288,384]{1,0:T(8,128)(2,1)S(1)}, u32[]{:S(2)}, u32[]{:S(2)}) %collective-permute-start.3) | collective-permute-done | bytes 221216 | tf_op jit(solution)/shard_map/ppermute | solution.py:414
  73.1 1.9 %shard_map.108.pre_ref = bf16[640,384]{1,0:T(8,128)(2,1)S(1)} custom-call(bf16[16,16,384]{2,1,0:T(8,128)(2,1)S(1)} %copy-done.1, bf16[288,384]{1,0:T(8,128)(2,1)S(1)} %collective-permute-done.2.left_ref, bf16[288,384]{1,0:T(8,128)(2,1)S(1)} %collective-permute-done.3.right_ref, bf16[80,384]{1,0:T(8,128)(2,1)S(1)} %collective-permute-done.above_ref, ...), custom_call_target="tpu_custom_call" | custom-call | flops 50000000 | bytes 340000 | tf_op jit(solution)/shard_map/pallas_call | solution.py:48
  75.1 0.0 copy-start.3
  75.1 0.6 shard_map.109.taps_ref
  75.7 12.9 %all-to-all-done.3.recv_ref = bf16[32,60,128]{2,1,0:T(8,128)(2,1)S(1)} async-done(((bf16[32,60,128]{2,1,0:T(8,128)(2,1)}), bf16[32,60,128]{2,1,0:T(8,128)(2,1)S(1)}, u32[]{:S(2)}, u32[]{:S(2)}) %all-to-all-start.3) | async-done | bytes 491552 | tf_op jit(solution)/shard_map/all_to_all | solution.py:418
  88.6 2.7 %shard_map.110 = bf16[16,16,384]{2,1,0:T(8,128)(2,1)} custom-call(s32[1]{0:T(128)} %bitcast.place_ref, bf16[32,60,128]{2,1,0:T(8,128)(2,1)S(1)} %all-to-all-done.3.recv_ref, bf16[640,384]{1,0:T(8,128)(2,1)S(1)} %shard_map.108.pre_ref, f32[3,16,256]{2,1,0:T(8,128)S(1)} %shard_map.109.taps_ref, f32[1,384]{1,0:T(1,128)S(1)} %broadcast_in_dim.19.norm_ref, ...), custom_call_target="tpu_custom_call" | custom-call | flops 1350000000 | bytes 9180000 | tf_op jit(solution)/shard_map/pallas_call | solution.py:48
  (29 shorter events, 0.2 us)
Async XLA Ops:
  0.0 17.4 %copy-start.1 = (bf16[16,16,384]{2,1,0:T(8,128)(2,1)S(1)}, bf16[16,16,384]{2,1,0:T(8,128)(2,1)}, u32[]{:S(2)}) copy-start(bf16[16,16,384]{2,1,0:T(8,128)(2,1)} %fields_ref.7) | copy-start | bytes 589828
  0.0 17.4 %copy-start.5 = (bf16[16,3,5,13]{3,0,2,1:T(8,128)(2,1)S(1)}, bf16[16,3,5,13]{3,0,2,1:T(8,128)(2,1)}, u32[]{:S(2)}) copy-start(bf16[16,3,5,13]{3,0,2,1:T(8,128)(2,1)} %param.12) | copy-start | bytes 18724
  0.0 17.4 %copy-start.7 = (s32[16]{0:T(128)S(1)}, s32[16]{0:T(128)}, u32[]{:S(2)}) copy-start(s32[16]{0:T(128)} %reach_ref.3) | copy-start | bytes 196
  2.0 28.6 %all-to-all-start = ((bf16[32,24,128]{2,1,0:T(8,128)(2,1)}), bf16[32,24,128]{2,1,0:T(8,128)(2,1)S(1)}, u32[]{:S(2)}, u32[]{:S(2)}) async-start(bf16[32,24,128]{2,1,0:T(8,128)(2,1)} %shard_map.100), calls=%async_computation | async-start | bytes 393216 | tf_op jit(solution)/shard_map/all_to_all | solution.py:418
  30.5 7.2 %copy-start.8 = (f32[192,12]{0,1:T(8,128)S(1)}, f32[192,12]{0,1:T(8,128)}, u32[]{:S(2)}) copy-start(f32[192,12]{0,1:T(8,128)} %param.11) | copy-start | bytes 27652
  32.0 11.4 %all-to-all-start.1 = ((bf16[16,48,128]{2,1,0:T(8,128)(2,1)}), bf16[16,48,128]{2,1,0:T(8,128)(2,1)S(1)}, u32[]{:S(2)}, u32[]{:S(2)}) async-start(bf16[16,48,128]{2,1,0:T(8,128)(2,1)} %shard_map.103), calls=%async_computation.1 | async-start | bytes 393216 | tf_op jit(solution)/shard_map/all_to_all | solution.py:418
  37.8 8.9 %collective-permute-start = (bf16[80,384]{1,0:T(8,128)(2,1)S(1)}, bf16[80,384]{1,0:T(8,128)(2,1)S(1)}, u32[]{:S(2)}, u32[]{:S(2)}) collective-permute-start(bf16[80,384]{1,0:T(8,128)(2,1)S(1)} %get-tuple-element.43), channel_id=1, source_target_pairs={{0,32},{32,64},{64,96},{96,128},{128,160},{160,192},{192,224},{224... | collective-permute-start | bytes 184328 | tf_op jit(solution)/shard_map/ppermute | solution.py:414
  39.9 6.9 %collective-permute-start.1 = (bf16[80,384]{1,0:T(8,128)(2,1)S(1)}, bf16[80,384]{1,0:T(8,128)(2,1)S(1)}, u32[]{:S(2)}, u32[]{:S(2)}) collective-permute-start(bf16[80,384]{1,0:T(8,128)(2,1)S(1)} %get-tuple-element.44), channel_id=1, source_target_pairs={{32,0},{64,32},{96,64},{128,96},{160,128},{192,160},{224,192},{256... | collective-permute-start | bytes 184328 | tf_op jit(solution)/shard_map/ppermute | solution.py:414
  46.7 16.2 %all-to-all-start.2 = ((bf16[16,48,128]{2,1,0:T(8,128)(2,1)}), bf16[16,48,128]{2,1,0:T(8,128)(2,1)S(1)}, u32[]{:S(2)}, u32[]{:S(2)}) async-start(bf16[16,48,128]{2,1,0:T(8,128)(2,1)} %shard_map.105), calls=%async_computation.2 | async-start | bytes 393216 | tf_op jit(solution)/shard_map/all_to_all | solution.py:418
  52.9 17.6 %collective-permute-start.2 = (bf16[288,384]{1,0:T(8,128)(2,1)S(1)}, bf16[288,384]{1,0:T(8,128)(2,1)S(1)}, u32[]{:S(2)}, u32[]{:S(2)}) collective-permute-start(bf16[288,384]{1,0:T(8,128)(2,1)S(1)} %get-tuple-element.52), channel_id=1, source_target_pairs={{0,1},{1,2},{2,3},{3,4},{4,5},{5,6},{6,7},{7,8},{8,9},{9,10},{10,1... | collective-permute-start | bytes 663560 | tf_op jit(solution)/shard_map/ppermute | solution.py:414
  56.3 16.8 %collective-permute-start.3 = (bf16[288,384]{1,0:T(8,128)(2,1)S(1)}, bf16[288,384]{1,0:T(8,128)(2,1)S(1)}, u32[]{:S(2)}, u32[]{:S(2)}) collective-permute-start(bf16[288,384]{1,0:T(8,128)(2,1)S(1)} %get-tuple-element.53), channel_id=1, source_target_pairs={{0,31},{1,0},{2,1},{3,2},{4,3},{5,4},{6,5},{7,6},{8,7},{9,8},{10,9... | collective-permute-start | bytes 663560 | tf_op jit(solution)/shard_map/ppermute | solution.py:414
  63.0 5.7 %copy-start.9 = (f32[384]{0:T(512)S(1)}, f32[384]{0:T(512)}, u32[]{:S(2)}) copy-start(f32[384]{0:T(512)} %param.17) | copy-start | bytes 4612
  64.7 8.4 %copy-start = (bf16[3,384,384]{2,1,0:T(8,128)(2,1)S(1)}, bf16[3,384,384]{2,1,0:T(8,128)(2,1)}, u32[]{:S(2)}) copy-start(bf16[3,384,384]{2,1,0:T(8,128)(2,1)} %mix_ref.2) | copy-start | bytes 2654212
  64.7 24.0 %all-to-all-start.3 = ((bf16[32,60,128]{2,1,0:T(8,128)(2,1)}), bf16[32,60,128]{2,1,0:T(8,128)(2,1)S(1)}, u32[]{:S(2)}, u32[]{:S(2)}) async-start(bf16[32,60,128]{2,1,0:T(8,128)(2,1)} %shard_map.106), calls=%async_computation.3 | async-start | bytes 1048576 | tf_op jit(solution)/shard_map/all_to_all | solution.py:418
  68.7 6.3 %copy-start.6 = (bf16[16,3,5,13]{3,0,2,1:T(8,128)(2,1)S(1)}, bf16[16,3,5,13]{3,0,2,1:T(8,128)(2,1)}, u32[]{:S(2)}) copy-start(bf16[16,3,5,13]{3,0,2,1:T(8,128)(2,1)} %param.13) | copy-start | bytes 18724
  75.0 13.6 %copy-start.2 = (bf16[3,384,384]{2,1,0:T(8,128)(2,1)S(1)}, bf16[3,384,384]{2,1,0:T(8,128)(2,1)}, u32[]{:S(2)}) copy-start(bf16[3,384,384]{2,1,0:T(8,128)(2,1)} %mix_ref.3) | copy-start | bytes 2654212
  75.1 13.6 %copy-start.3 = (bf16[384,768]{1,0:T(8,128)(2,1)S(1)}, bf16[384,768]{1,0:T(8,128)(2,1)}, u32[]{:S(2)}) copy-start(bf16[384,768]{1,0:T(8,128)(2,1)} %in_ref.1) | copy-start | bytes 1769476
  75.1 13.6 %copy-start.4 = (bf16[768,384]{1,0:T(8,128)(2,1)S(1)}, bf16[768,384]{1,0:T(8,128)(2,1)}, u32[]{:S(2)}) copy-start(bf16[768,384]{1,0:T(8,128)(2,1)} %back_ref.1) | copy-start | bytes 1769476

commit v5 on v3

--- a/solution.py
+++ b/solution.py
@@ -339,7 +339,7 @@
 
 def last_kernel(
     place_ref, recv_ref, pre_ref, taps_ref, norm_ref, mix_ref, in_ref, back_ref, out_ref,
-    rows, stream, exact, gathered,
+    rows, stream, gathered,
 ):
     place = place_ref[0]
     for s in range(PLON):
@@ -350,10 +350,13 @@
         row = lax.broadcasted_iota(jnp.int32, (128, C), 0) // JX + 4 * hi - RLAT + place * A
         value = jnp.where((row >= 0) & (row < NLAT), value, 0.0).astype(BF)
         stream[128 * hi : 128 * hi + 128, :] = value
-        exact[128 * hi : 128 * hi + 128, :] = value.astype(F32)
     second = gather_rows(taps_ref, stream, mix_ref, gathered, A, N, JX, OFF - RLON)
     own = jnp.concatenate(
-        [exact[(a + RLAT) * JX + OFF : (a + RLAT) * JX + OFF + N, :] for a in range(A)], axis=0
+        [
+            stream[(a + RLAT) * JX : (a + RLAT + 1) * JX, :].astype(F32)[OFF : OFF + N]
+            for a in range(A)
+        ],
+        axis=0,
     )
     summed = own + second
     center = summed - jnp.mean(summed, axis=-1, keepdims=True)
@@ -536,7 +539,6 @@
         [
             pltpu.VMEM((1920, 128), F32),
             pltpu.VMEM((AX * JX, C), BF),
-            pltpu.VMEM((AX * JX, C), F32),
             pltpu.VMEM((KB, A * N, C), BF),
         ],
         place.reshape(1),

time: 92 us -> 91.9 us (level)
  no operation moved by 1% of the time
where the time goes in v5:
time: 91.9 us; the launch traced here: 91.3 us
  starting transfers between devices  46.5 us (51%)
  waiting for transfers between devices  25.9 us (28%)
  Pallas kernels  18 us (20%)
    all_to_all x4, starting transfers between devices, exchange(): return lax.all_to_all(block, axis, split_axis=0, concat_axis=0, tiled=True)  30.9 us
    all_to_all x4, waiting for transfers between devices, exchange(): return lax.all_to_all(block, axis, split_axis=0, concat_axis=0, tiled=True)  21.5 us
    pallas_call x11, Pallas kernels, call(): pl.pallas_call(kernel, out_shape=outs, in_specs=specs, out_specs=out_spec...  18 us
    ppermute x4, starting transfers between devices, shifted(): return lax.ppermute(value, axis, pairs)  15.6 us
    ppermute x4, waiting for transfers between devices, shifted(): return lax.ppermute(value, axis, pairs)  4.42 us
  transfers between devices with their start and end apart: 8, of which 4 were waited for; matrix products, arithmetic and copies ran while one was open for 1% of the time, Pallas kernels for 13%

profile of v5, /device:TPU:12, one launch (start us, length us, event | category | flops | bytes accessed | tf_op | source)
XLA Modules:
  0.0 91.3 jit_solution(2613583723788260335)
XLA Ops:
  0.0 0.0 copy-start.7
  0.0 1.9 %shard_map.100 = bf16[32,24,128]{2,1,0:T(8,128)(2,1)} custom-call(bf16[16,16,384]{2,1,0:T(8,128)(2,1)} %fields_ref.7), custom_call_target="tpu_custom_call" | custom-call | flops 550000000 | bytes 3740000 | tf_op jit(solution)/shard_map/pallas_call | solution.py:48
  2.0 15.1 %all-to-all-start = ((bf16[32,24,128]{2,1,0:T(8,128)(2,1)}), bf16[32,24,128]{2,1,0:T(8,128)(2,1)S(1)}, u32[]{:S(2)}, u32[]{:S(2)}) async-start(bf16[32,24,128]{2,1,0:T(8,128)(2,1)} %shard_map.100), calls=%async_computation | async-start | bytes 393216 | tf_op jit(solution)/shard_map/all_to_all | solution.py:389
  17.1 0.1 fusion.1.cos_ref
  17.2 0.2 select_reduce_fusion
  17.4 0.7 shard_map.104
  18.1 0.4 shard_map.102
  18.5 0.1 add_exponential_fusion.diag_ref
  18.6 0.1 broadcast_in_dim.16.order_ref
  18.6 3.2 %shard_map.101.tab_ref = bf16[12,192,256]{2,1,0:T(8,128)(2,1)S(1)} custom-call(f32[16,128]{1,0:T(8,128)S(1)} %broadcast_in_dim.16.order_ref, f32[1,256]{1,0:T(1,128)S(1)} %fusion.1.cos_ref, f32[16,256]{1,0:T(8,128)S(1)} %add_exponential_fusion.diag_ref), custom_call_target="tpu_custom_call" | custom-call | flops 1650000000 | bytes 11220000 | tf_op jit(solution)/shard_map/pallas_call | solution.py:48
  21.9 8.6 %all-to-all-done.recv_ref = bf16[32,24,128]{2,1,0:T(8,128)(2,1)S(1)} async-done(((bf16[32,24,128]{2,1,0:T(8,128)(2,1)}), bf16[32,24,128]{2,1,0:T(8,128)(2,1)S(1)}, u32[]{:S(2)}, u32[]{:S(2)}) %all-to-all-start) | async-done | bytes 196640 | tf_op jit(solution)/shard_map/all_to_all | solution.py:389
  30.5 1.4 %shard_map.103 = bf16[16,48,128]{2,1,0:T(8,128)(2,1)} custom-call(bf16[32,24,128]{2,1,0:T(8,128)(2,1)S(1)} %all-to-all-done.recv_ref, f32[32,384]{1,0:T(8,128)S(1)} %get-tuple-element.35.u_ref, f32[32,384]{1,0:T(8,128)S(1)} %get-tuple-element.36.v_ref, f32[16,384]{1,0:T(8,128)S(1)} %get-tuple-element.37.c_ref, f32[16,384]{1,0:T(8,128)S(1)} %get-tuple-element.38.s_ref), custom_call_target="tpu_custom_call" | custom-call | flops 700000000 | bytes 4760000 | tf_op jit(solution)/shard_map/pallas_call | solution.py:48
  31.9 5.7 %all-to-all-start.1 = ((bf16[16,48,128]{2,1,0:T(8,128)(2,1)}), bf16[16,48,128]{2,1,0:T(8,128)(2,1)S(1)}, u32[]{:S(2)}, u32[]{:S(2)}) async-start(bf16[16,48,128]{2,1,0:T(8,128)(2,1)} %shard_map.103), calls=%async_computation.1 | async-start | bytes 393216 | tf_op jit(solution)/shard_map/all_to_all | solution.py:389
  37.7 0.1 sine_multiply_fusion.quad_ref
  37.7 2.1 %collective-permute-start = (bf16[80,384]{1,0:T(8,128)(2,1)S(1)}, bf16[80,384]{1,0:T(8,128)(2,1)S(1)}, u32[]{:S(2)}, u32[]{:S(2)}) collective-permute-start(bf16[80,384]{1,0:T(8,128)(2,1)S(1)} %get-tuple-element.43), channel_id=1, source_target_pairs={{0,32},{32,64},{64,96},{96,128},{128,160},{160,192},{192,224},{224... | collective-permute-start | bytes 184328 | tf_op jit(solution)/shard_map/ppermute | solution.py:385
  39.8 3.5 %collective-permute-start.1 = (bf16[80,384]{1,0:T(8,128)(2,1)S(1)}, bf16[80,384]{1,0:T(8,128)(2,1)S(1)}, u32[]{:S(2)}, u32[]{:S(2)}) collective-permute-start(bf16[80,384]{1,0:T(8,128)(2,1)S(1)} %get-tuple-element.44), channel_id=1, source_target_pairs={{32,0},{64,32},{96,64},{128,96},{160,128},{192,160},{224,192},{256... | collective-permute-start | bytes 184328 | tf_op jit(solution)/shard_map/ppermute | solution.py:385
  43.3 3.3 %shard_map.105 = bf16[16,48,128]{2,1,0:T(8,128)(2,1)} custom-call(bf16[16,48,128]{2,1,0:T(8,128)(2,1)S(1)} %all-to-all-done.1.recv_ref, bf16[12,192,256]{2,1,0:T(8,128)(2,1)S(1)} %shard_map.101.tab_ref, f32[1,256]{1,0:T(1,128)S(1)} %sine_multiply_fusion.quad_ref, f32[32,192]{1,0:T(8,128)S(1)} %pad_maximum_fusion.gain_ref), custom_call_target="tpu_custom_call" | custom-call | flops 1300000000 | bytes 8840000 | tf_op jit(solution)/shard_map/pallas_call | solution.py:48
  46.7 6.0 %all-to-all-start.2 = ((bf16[16,48,128]{2,1,0:T(8,128)(2,1)}), bf16[16,48,128]{2,1,0:T(8,128)(2,1)S(1)}, u32[]{:S(2)}, u32[]{:S(2)}) async-start(bf16[16,48,128]{2,1,0:T(8,128)(2,1)} %shard_map.105), calls=%async_computation.2 | async-start | bytes 393216 | tf_op jit(solution)/shard_map/all_to_all | solution.py:389
  52.7 0.1 shard_map.107
  52.8 3.4 %collective-permute-start.2 = (bf16[288,384]{1,0:T(8,128)(2,1)S(1)}, bf16[288,384]{1,0:T(8,128)(2,1)S(1)}, u32[]{:S(2)}, u32[]{:S(2)}) collective-permute-start(bf16[288,384]{1,0:T(8,128)(2,1)S(1)} %get-tuple-element.52), channel_id=1, source_target_pairs={{0,1},{1,2},{2,3},{3,4},{4,5},{5,6},{6,7},{7,8},{8,9},{9,10},{10,1... | collective-permute-start | bytes 663560 | tf_op jit(solution)/shard_map/ppermute | solution.py:385
  56.2 6.7 %collective-permute-start.3 = (bf16[288,384]{1,0:T(8,128)(2,1)S(1)}, bf16[288,384]{1,0:T(8,128)(2,1)S(1)}, u32[]{:S(2)}, u32[]{:S(2)}) collective-permute-start(bf16[288,384]{1,0:T(8,128)(2,1)S(1)} %get-tuple-element.53), channel_id=1, source_target_pairs={{0,31},{1,0},{2,1},{3,2},{4,3},{5,4},{6,5},{7,6},{8,7},{9,8},{10,9... | collective-permute-start | bytes 663560 | tf_op jit(solution)/shard_map/ppermute | solution.py:385
  62.9 0.0 copy-start.9
  62.9 1.8 %shard_map.106 = bf16[32,60,128]{2,1,0:T(8,128)(2,1)} custom-call(bf16[16,48,128]{2,1,0:T(8,128)(2,1)S(1)} %all-to-all-done.2.recv_ref, f32[32,384]{1,0:T(8,128)S(1)} %get-tuple-element.46.u_ref, f32[32,384]{1,0:T(8,128)S(1)} %get-tuple-element.47.v_ref, f32[32,384]{1,0:T(8,128)S(1)} %get-tuple-element.48.c_ref, f32[32,384]{1,0:T(8,128)S(1)} %get-tuple-element.49.s_ref), custom_call_target="tpu_custom_call" | custom-call | flops 850000000 | bytes 5780000 | tf_op jit(solution)/shard_map/pallas_call | solution.py:48
  64.7 4.0 %all-to-all-start.3 = ((bf16[32,60,128]{2,1,0:T(8,128)(2,1)}), bf16[32,60,128]{2,1,0:T(8,128)(2,1)S(1)}, u32[]{:S(2)}, u32[]{:S(2)}) async-start(bf16[32,60,128]{2,1,0:T(8,128)(2,1)} %shard_map.106), calls=%async_computation.3 | async-start | bytes 1048576 | tf_op jit(solution)/shard_map/all_to_all | solution.py:389
  68.7 0.0 copy-start.6
  68.8 1.7 %collective-permute-done.2.left_ref = bf16[288,384]{1,0:T(8,128)(2,1)S(1)} collective-permute-done((bf16[288,384]{1,0:T(8,128)(2,1)S(1)}, bf16[288,384]{1,0:T(8,128)(2,1)S(1)}, u32[]{:S(2)}, u32[]{:S(2)}) %collective-permute-start.2) | collective-permute-done | bytes 221216 | tf_op jit(solution)/shard_map/ppermute | solution.py:385
  70.4 2.7 %collective-permute-done.3.right_ref = bf16[288,384]{1,0:T(8,128)(2,1)S(1)} collective-permute-done((bf16[288,384]{1,0:T(8,128)(2,1)S(1)}, bf16[288,384]{1,0:T(8,128)(2,1)S(1)}, u32[]{:S(2)}, u32[]{:S(2)}) %collective-permute-start.3) | collective-permute-done | bytes 221216 | tf_op jit(solution)/shard_map/ppermute | solution.py:385
  73.2 1.9 %shard_map.108.pre_ref = bf16[640,384]{1,0:T(8,128)(2,1)S(1)} custom-call(bf16[16,16,384]{2,1,0:T(8,128)(2,1)S(1)} %copy-done.1, bf16[288,384]{1,0:T(8,128)(2,1)S(1)} %collective-permute-done.2.left_ref, bf16[288,384]{1,0:T(8,128)(2,1)S(1)} %collective-permute-done.3.right_ref, bf16[80,384]{1,0:T(8,128)(2,1)S(1)} %collective-permute-done.above_ref, ...), custom_call_target="tpu_custom_call" | custom-call | flops 50000000 | bytes 340000 | tf_op jit(solution)/shard_map/pallas_call | solution.py:48
  75.1 0.0 copy-start.4
  75.1 0.6 shard_map.109.taps_ref
  75.8 12.8 %all-to-all-done.3.recv_ref = bf16[32,60,128]{2,1,0:T(8,128)(2,1)S(1)} async-done(((bf16[32,60,128]{2,1,0:T(8,128)(2,1)}), bf16[32,60,128]{2,1,0:T(8,128)(2,1)S(1)}, u32[]{:S(2)}, u32[]{:S(2)}) %all-to-all-start.3) | async-done | bytes 491552 | tf_op jit(solution)/shard_map/all_to_all | solution.py:389
  88.6 2.7 %shard_map.110 = bf16[16,16,384]{2,1,0:T(8,128)(2,1)} custom-call(s32[1]{0:T(128)} %bitcast.place_ref, bf16[32,60,128]{2,1,0:T(8,128)(2,1)S(1)} %all-to-all-done.3.recv_ref, bf16[640,384]{1,0:T(8,128)(2,1)S(1)} %shard_map.108.pre_ref, f32[3,16,256]{2,1,0:T(8,128)S(1)} %shard_map.109.taps_ref, f32[1,384]{1,0:T(1,128)S(1)} %broadcast_in_dim.19.norm_ref, ...), custom_call_target="tpu_custom_call" | custom-call | flops 1350000000 | bytes 9180000 | tf_op jit(solution)/shard_map/pallas_call | solution.py:48
  (29 shorter events, 0.2 us)
Async XLA Ops:
  0.0 17.4 %copy-start.1 = (bf16[16,16,384]{2,1,0:T(8,128)(2,1)S(1)}, bf16[16,16,384]{2,1,0:T(8,128)(2,1)}, u32[]{:S(2)}) copy-start(bf16[16,16,384]{2,1,0:T(8,128)(2,1)} %fields_ref.7) | copy-start | bytes 589828
  0.0 17.4 %copy-start.5 = (bf16[16,3,5,13]{3,0,2,1:T(8,128)(2,1)S(1)}, bf16[16,3,5,13]{3,0,2,1:T(8,128)(2,1)}, u32[]{:S(2)}) copy-start(bf16[16,3,5,13]{3,0,2,1:T(8,128)(2,1)} %param.12) | copy-start | bytes 18724
  0.0 17.4 %copy-start.7 = (s32[16]{0:T(128)S(1)}, s32[16]{0:T(128)}, u32[]{:S(2)}) copy-start(s32[16]{0:T(128)} %reach_ref.3) | copy-start | bytes 196
  2.0 28.6 %all-to-all-start = ((bf16[32,24,128]{2,1,0:T(8,128)(2,1)}), bf16[32,24,128]{2,1,0:T(8,128)(2,1)S(1)}, u32[]{:S(2)}, u32[]{:S(2)}) async-start(bf16[32,24,128]{2,1,0:T(8,128)(2,1)} %shard_map.100), calls=%async_computation | async-start | bytes 393216 | tf_op jit(solution)/shard_map/all_to_all | solution.py:389
  30.5 7.1 %copy-start.8 = (f32[192,12]{0,1:T(8,128)S(1)}, f32[192,12]{0,1:T(8,128)}, u32[]{:S(2)}) copy-start(f32[192,12]{0,1:T(8,128)} %param.11) | copy-start | bytes 27652
  31.9 11.4 %all-to-all-start.1 = ((bf16[16,48,128]{2,1,0:T(8,128)(2,1)}), bf16[16,48,128]{2,1,0:T(8,128)(2,1)S(1)}, u32[]{:S(2)}, u32[]{:S(2)}) async-start(bf16[16,48,128]{2,1,0:T(8,128)(2,1)} %shard_map.103), calls=%async_computation.1 | async-start | bytes 393216 | tf_op jit(solution)/shard_map/all_to_all | solution.py:389
  37.7 8.9 %collective-permute-start = (bf16[80,384]{1,0:T(8,128)(2,1)S(1)}, bf16[80,384]{1,0:T(8,128)(2,1)S(1)}, u32[]{:S(2)}, u32[]{:S(2)}) collective-permute-start(bf16[80,384]{1,0:T(8,128)(2,1)S(1)} %get-tuple-element.43), channel_id=1, source_target_pairs={{0,32},{32,64},{64,96},{96,128},{128,160},{160,192},{192,224},{224... | collective-permute-start | bytes 184328 | tf_op jit(solution)/shard_map/ppermute | solution.py:385
  39.8 6.9 %collective-permute-start.1 = (bf16[80,384]{1,0:T(8,128)(2,1)S(1)}, bf16[80,384]{1,0:T(8,128)(2,1)S(1)}, u32[]{:S(2)}, u32[]{:S(2)}) collective-permute-start(bf16[80,384]{1,0:T(8,128)(2,1)S(1)} %get-tuple-element.44), channel_id=1, source_target_pairs={{32,0},{64,32},{96,64},{128,96},{160,128},{192,160},{224,192},{256... | collective-permute-start | bytes 184328 | tf_op jit(solution)/shard_map/ppermute | solution.py:385
  46.7 16.2 %all-to-all-start.2 = ((bf16[16,48,128]{2,1,0:T(8,128)(2,1)}), bf16[16,48,128]{2,1,0:T(8,128)(2,1)S(1)}, u32[]{:S(2)}, u32[]{:S(2)}) async-start(bf16[16,48,128]{2,1,0:T(8,128)(2,1)} %shard_map.105), calls=%async_computation.2 | async-start | bytes 393216 | tf_op jit(solution)/shard_map/all_to_all | solution.py:389
  52.8 17.6 %collective-permute-start.2 = (bf16[288,384]{1,0:T(8,128)(2,1)S(1)}, bf16[288,384]{1,0:T(8,128)(2,1)S(1)}, u32[]{:S(2)}, u32[]{:S(2)}) collective-permute-start(bf16[288,384]{1,0:T(8,128)(2,1)S(1)} %get-tuple-element.52), channel_id=1, source_target_pairs={{0,1},{1,2},{2,3},{3,4},{4,5},{5,6},{6,7},{7,8},{8,9},{9,10},{10,1... | collective-permute-start | bytes 663560 | tf_op jit(solution)/shard_map/ppermute | solution.py:385
  56.2 16.9 %collective-permute-start.3 = (bf16[288,384]{1,0:T(8,128)(2,1)S(1)}, bf16[288,384]{1,0:T(8,128)(2,1)S(1)}, u32[]{:S(2)}, u32[]{:S(2)}) collective-permute-start(bf16[288,384]{1,0:T(8,128)(2,1)S(1)} %get-tuple-element.53), channel_id=1, source_target_pairs={{0,31},{1,0},{2,1},{3,2},{4,3},{5,4},{6,5},{7,6},{8,7},{9,8},{10,9... | collective-permute-start | bytes 663560 | tf_op jit(solution)/shard_map/ppermute | solution.py:385
  62.9 5.8 %copy-start.9 = (f32[384]{0:T(512)S(1)}, f32[384]{0:T(512)}, u32[]{:S(2)}) copy-start(f32[384]{0:T(512)} %param.17) | copy-start | bytes 4612
  64.7 8.5 %copy-start = (bf16[3,384,384]{2,1,0:T(8,128)(2,1)S(1)}, bf16[3,384,384]{2,1,0:T(8,128)(2,1)}, u32[]{:S(2)}) copy-start(bf16[3,384,384]{2,1,0:T(8,128)(2,1)} %mix_ref.2) | copy-start | bytes 2654212
  64.7 23.9 %all-to-all-start.3 = ((bf16[32,60,128]{2,1,0:T(8,128)(2,1)}), bf16[32,60,128]{2,1,0:T(8,128)(2,1)S(1)}, u32[]{:S(2)}, u32[]{:S(2)}) async-start(bf16[32,60,128]{2,1,0:T(8,128)(2,1)} %shard_map.106), calls=%async_computation.3 | async-start | bytes 1048576 | tf_op jit(solution)/shard_map/all_to_all | solution.py:389
  68.7 6.4 %copy-start.6 = (bf16[16,3,5,13]{3,0,2,1:T(8,128)(2,1)S(1)}, bf16[16,3,5,13]{3,0,2,1:T(8,128)(2,1)}, u32[]{:S(2)}) copy-start(bf16[16,3,5,13]{3,0,2,1:T(8,128)(2,1)} %param.13) | copy-start | bytes 18724
  75.1 13.5 %copy-start.2 = (bf16[3,384,384]{2,1,0:T(8,128)(2,1)S(1)}, bf16[3,384,384]{2,1,0:T(8,128)(2,1)}, u32[]{:S(2)}) copy-start(bf16[3,384,384]{2,1,0:T(8,128)(2,1)} %mix_ref.3) | copy-start | bytes 2654212
  75.1 13.5 %copy-start.3 = (bf16[384,768]{1,0:T(8,128)(2,1)S(1)}, bf16[384,768]{1,0:T(8,128)(2,1)}, u32[]{:S(2)}) copy-start(bf16[384,768]{1,0:T(8,128)(2,1)} %in_ref.1) | copy-start | bytes 1769476
  75.1 13.5 %copy-start.4 = (bf16[768,384]{1,0:T(8,128)(2,1)S(1)}, bf16[768,384]{1,0:T(8,128)(2,1)}, u32[]{:S(2)}) copy-start(bf16[768,384]{1,0:T(8,128)(2,1)} %back_ref.1) | copy-start | bytes 1769476
